TPU v7x, 32 devices: a whole 2x2x4 slice. The times are simulated.
32 devices in a mesh: wide: 8 (over z, x), narrow: 4 (over y, core).
Axes of the slice: x: 2, y: 2, z: 4, core: 2. Of those that a mesh axis runs over, the one named last changes fastest.
Arguments:
- aperture: float32 [64, 128, 128], P(('wide', 'narrow')), may hold values from 0.8 to 2.5
- pressure: float32 [64, 128, 128], P(('wide', 'narrow')), may hold values from -6 to 6
- adj_source: float32 [64, 128, 128], P(('wide', 'narrow')), may hold values from -6 to 6
- trace_weight: float32 [512, 64], P(('wide', 'narrow')), may hold values from 0.2 to 2
- end_device: int32 [512, 2], P(('wide', 'narrow')), may hold values from 0 to 31, as said below
- end_local: int32 [512, 2], P(('wide', 'narrow')), may hold values from 0 to 1
- trace_nodes: int32 [512, 2, 64], P(('wide', 'narrow')), may hold values from 0 to 16383
Outputs:
- aperture_grad: float32 [64, 128, 128], P(('wide', 'narrow'))
- adjoint: float32 [64, 128, 128], P(('wide', 'narrow'))
Inputs may be any that keep to these rules, and one draw needn't show every extreme that they name: `end_device`: the two ends of an intersection lie on different devices. Of the ends of the intersections owned by one device, every device holds none or exactly 2. Any two devices are joined by at most 2 intersections over all owners, and some pairs by exactly 2. `trace_nodes`: several trace nodes may share a cell.
All inputs are finite; a program needn't handle non-finite values.
Results may differ from a plain program's by a relative error of at most 0.0022.
Values sent between devices are 32-bit elements; how exact they have to be, the bound alone decides.
No kernel may reach another device: no remote copies, remote signals or barrier semaphores. Data moves between devices by JAX's collectives and lax.ppermute only.
A program may use at most 64 MiB of HBM per device.

v0:
```python
import jax
import jax.numpy as jnp
from jax import lax
from jax.sharding import PartitionSpec as P

SWEEPS = 3
INNER = 8


LEAKAGE = 0.25
HIGH = lax.Precision.HIGHEST


def neighbours(field, face_x, face_y):
    total = jnp.pad(face_x * field[:, 1:, :], ((0, 0), (0, 1), (0, 0)))
    total = total + jnp.pad(face_x * field[:, :-1, :], ((0, 0), (1, 0), (0, 0)))
    total = total + jnp.pad(face_y * field[:, :, 1:], ((0, 0), (0, 0), (0, 1)))
    total = total + jnp.pad(face_y * field[:, :, :-1], ((0, 0), (0, 0), (1, 0)))
    return total


def face_total(face_x, face_y):
    total = jnp.pad(face_x, ((0, 0), (0, 1), (0, 0))) + jnp.pad(face_x, ((0, 0), (1, 0), (0, 0)))
    return (
        total
        + jnp.pad(face_y, ((0, 0), (0, 0), (0, 1)))
        + jnp.pad(face_y, ((0, 0), (0, 0), (1, 0)))
    )


def gradient_of(aperture, pressure, adjoint):
    along_x = (pressure[:, 1:, :] - pressure[:, :-1, :]) * (adjoint[:, 1:, :] - adjoint[:, :-1, :])
    along_y = (pressure[:, :, 1:] - pressure[:, :, :-1]) * (adjoint[:, :, 1:] - adjoint[:, :, :-1])
    return -(aperture * aperture / 8.0) * face_total(along_x, along_y)


def rank_within(target, device_count):
    member = (target[:, None] == jnp.arange(device_count, dtype=jnp.int32)[None, :]).astype(
        jnp.int32
    )
    before = jnp.cumsum(member, axis=0) - member
    return jnp.sum(before * member, axis=1)


def split_pair(values):
    high_part = values.astype(jnp.bfloat16)
    low_part = (values - high_part.astype(jnp.float32)).astype(jnp.bfloat16)
    return (high_part, low_part)


def group_size(device_count, width):
    group = 1
    while device_count % (group * 2) == 0 and group * 2 * width <= 2048:
        group = group * 2
    return group


def scatter_cells(row_index, col_index, values, row_count, grid_size, blocks):
    row_blocks = row_index.reshape(blocks, -1)
    col_blocks = col_index.reshape(blocks, -1)
    value_blocks = values.reshape(blocks, -1)
    row_ids = jnp.arange(row_count, dtype=jnp.int32)
    col_ids = jnp.arange(grid_size, dtype=jnp.int32)
    zero_half = jnp.zeros((), jnp.bfloat16)

    def add_block(total, pieces):
        rows_now, cols_now, vals_now = pieces
        row_hot = (rows_now[None, :] == row_ids[:, None]).astype(jnp.bfloat16)
        col_hot = cols_now[:, None] == col_ids[None, :]
        high_part, low_part = split_pair(vals_now)
        right = jnp.concatenate(
            [
                jnp.where(col_hot, high_part[:, None], zero_half),
                jnp.where(col_hot, low_part[:, None], zero_half),
            ],
            axis=1,
        )
        product = jnp.dot(row_hot, right, preferred_element_type=jnp.float32)
        return (total + product[:, :grid_size] + product[:, grid_size:], None)

    start = jnp.zeros((row_count, grid_size), jnp.float32)
    total, _ = lax.scan(add_block, start, (row_blocks, col_blocks, value_blocks))
    return total


def gather_cells(field_rows, row_index, col_index, blocks):
    row_count, grid_size = field_rows.shape
    high_part, low_part = split_pair(field_rows)
    both_parts = jnp.concatenate([high_part, low_part], axis=1)
    row_ids = jnp.arange(row_count, dtype=jnp.int32)
    col_ids = jnp.arange(grid_size, dtype=jnp.int32)

    def pick_block(carry, pieces):
        rows_now, cols_now = pieces
        row_hot = (rows_now[:, None] == row_ids[None, :]).astype(jnp.bfloat16)
        picked = jnp.dot(row_hot, both_parts, preferred_element_type=jnp.float32)
        merged = picked[:, :grid_size] + picked[:, grid_size:]
        col_hot = cols_now[:, None] == col_ids[None, :]
        return (carry, jnp.sum(jnp.where(col_hot, merged, 0.0), axis=1))

    _, picked_all = lax.scan(
        pick_block, 0, (row_index.reshape(blocks, -1), col_index.reshape(blocks, -1))
    )
    return picked_all.reshape(-1)


def body(aperture, pressure, adj_source, trace_weight, end_device, end_local, trace_nodes):
    frac_count, grid_size, _ = aperture.shape
    owned_count, trace_len = trace_weight.shape
    device_count = lax.axis_size(("wide", "narrow"))
    capacity = owned_count // (device_count // 4)
    end_count = 2 * owned_count
    slot_total = device_count * capacity
    row_width = capacity * trace_len
    blocks = device_count // group_size(device_count, row_width)
    row_count = frac_count * grid_size
    conduct = aperture * aperture * aperture / 12.0
    face_x = (conduct[:, :-1, :] + conduct[:, 1:, :]) * 0.5
    face_y = (conduct[:, :, :-1] + conduct[:, :, 1:]) * 0.5
    destination = end_device.reshape(end_count)
    slot_place = destination * capacity + rank_within(destination, device_count)
    placing = (slot_place[:, None] == jnp.arange(slot_total, dtype=jnp.int32)[None, :]).astype(
        jnp.float32
    )
    cells_own = end_local.reshape(end_count, 1) * (grid_size * grid_size) + trace_nodes.reshape(
        end_count, trace_len
    )
    outgoing = jnp.full((slot_total, trace_len), -1, jnp.int32).at[slot_place].set(cells_own)
    outgoing = outgoing.reshape(device_count, row_width)
    weight_end = jnp.broadcast_to(trace_weight[:, None, :], (owned_count, 2, trace_len)).reshape(
        end_count, trace_len
    )
    weight_out = jnp.einsum("es,et->st", placing, weight_end, precision=HIGH)
    weight_out = weight_out.reshape(device_count, row_width)
    incoming = lax.all_to_all(outgoing, ("wide", "narrow"), split_axis=0, concat_axis=0, tiled=True)
    weight_in = lax.all_to_all(
        weight_out, ("wide", "narrow"), split_axis=0, concat_axis=0, tiled=True
    )
    active_slot = (incoming >= 0).reshape(-1)
    flat_cells = incoming.reshape(-1)
    row_index = jnp.where(active_slot, flat_cells // grid_size, -1)
    col_index = jnp.where(active_slot, flat_cells % grid_size, -1)
    trace_sum = scatter_cells(
        row_index,
        col_index,
        jnp.where(active_slot, weight_in.reshape(-1), 0.0),
        row_count,
        grid_size,
        blocks,
    ).reshape(frac_count, grid_size, grid_size)
    inv_diag = 1.0 / (LEAKAGE + face_total(face_x, face_y) + trace_sum)
    adjoint = adj_source * inv_diag
    for sweep_step in range(SWEEPS):
        values = gather_cells(adjoint.reshape(row_count, grid_size), row_index, col_index, blocks)
        values = values.reshape(device_count, row_width)
        returned = lax.all_to_all(
            values, ("wide", "narrow"), split_axis=0, concat_axis=0, tiled=True
        )
        end_values = jnp.dot(placing, returned.reshape(slot_total, trace_len), precision=HIGH)
        end_values = end_values.reshape(owned_count, 2, trace_len)
        source_end = (trace_weight[:, None, :] * end_values[:, ::-1, :]).reshape(
            end_count, trace_len
        )
        packed = jnp.einsum("es,et->st", placing, source_end, precision=HIGH)
        packed = packed.reshape(device_count, row_width)
        arrived = lax.all_to_all(
            packed, ("wide", "narrow"), split_axis=0, concat_axis=0, tiled=True
        )
        coupling = scatter_cells(
            row_index,
            col_index,
            jnp.where(active_slot, arrived.reshape(-1), 0.0),
            row_count,
            grid_size,
            blocks,
        ).reshape(frac_count, grid_size, grid_size)
        forcing = adj_source + coupling
        for inner_step in range(INNER):
            adjoint = (forcing + neighbours(adjoint, face_x, face_y)) * inv_diag
    return (gradient_of(aperture, pressure, adjoint), adjoint)


def solution(mesh):
    placed = (
        P(("wide", "narrow"), None, None),
        P(("wide", "narrow"), None, None),
        P(("wide", "narrow"), None, None),
        P(("wide", "narrow"), None),
        P(("wide", "narrow"), None),
        P(("wide", "narrow"), None),
        P(("wide", "narrow"), None, None),
    )
    return jax.shard_map(
        body,
        mesh=mesh,
        in_specs=placed,
        out_specs=(P(("wide", "narrow"), None, None), P(("wide", "narrow"), None, None)),
        check_vma=False,
    )
```

profile of v0, /device:TPU:0, one launch (start us, length us, event | category | flops | bytes accessed | tf_op | source)
XLA Modules:
  0.0 130.8 jit_solution(4801494080324948352)
XLA Ops:
  0.6 0.8 copy.21
  1.8 0.7 mul.462.clone
  2.8 0.7 all_to_all.53
  3.5 7.3 %all-to-all-start.1 = ((f32[32,1,128]{2,1,0:T(1,128)}), f32[32,1,128]{2,1,0:T(1,128)S(1)}, u32[]{:S(2)}, u32[]{:S(2)}) async-start(f32[32,1,128]{2,1,0:T(1,128)} %bitcast.5), calls=%async_computation.1 | async-start | bytes 32768 | tf_op jit(solution)/shard_map/all_to_all | solution.py:136
  11.0 0.7 broadcast_multiply_fusion.1
  11.7 0.9 fusion.74
  12.9 0.9 scatter_custom_fusion
  13.8 0.7 all_to_all.50
  14.5 3.3 %all-to-all-done.1 = f32[32,1,128]{2,1,0:T(1,128)S(1)} async-done(((f32[32,1,128]{2,1,0:T(1,128)}), f32[32,1,128]{2,1,0:T(1,128)S(1)}, u32[]{:S(2)}, u32[]{:S(2)}) %all-to-all-start.1) | async-done | bytes 16416 | tf_op jit(solution)/shard_map/all_to_all | solution.py:136
  17.9 2.5 %all-to-all-start = ((s32[32,1,128]{2,1,0:T(1,128)}), s32[32,1,128]{2,1,0:T(1,128)S(1)}, u32[]{:S(2)}, u32[]{:S(2)}) async-start(s32[32,1,128]{2,1,0:T(1,128)} %all_to_all.50), calls=%async_computation | async-start | bytes 32768 | tf_op jit(solution)/shard_map/all_to_all | solution.py:135
  20.6 0.5 broadcast.397
  21.1 0.6 reduce.25
  21.7 5.8 %all-to-all-done = s32[32,1,128]{2,1,0:T(1,128)S(1)} async-done(((s32[32,1,128]{2,1,0:T(1,128)}), s32[32,1,128]{2,1,0:T(1,128)S(1)}, u32[]{:S(2)}, u32[]{:S(2)}) %all-to-all-start) | async-done | bytes 16416 | tf_op jit(solution)/shard_map/all_to_all | solution.py:135
  27.5 0.5 broadcast.396
  28.0 0.7 reduce.24
  28.8 4.5 %while.80 = (s32[]{:T(128)}, f32[256,128]{1,0:T(8,128)S(1)}, s32[2,2048]{1,0:T(2,128)S(1)}, s32[2,2048]{1,0:T(2,128)S(1)}, f32[2,2048]{1,0:T(2,128)S(1)}, /*index=5*/s32[]{:T(128)}, s32[]{:T(128)}) while((s32[]{:T(128)}, f32[256,128]{1,0:T(8,128)S(1)}, s32[2,2048]{1,0:T(2,128)S(1)}, s32[2,2048]{1,0:T(2,128)S(1)}, ...), condition=%wide.region_4.5_spmd.clone, body=%wide.region_3.4_spmd.clone.sunk | while | flops 271949824 | bytes 2973791 | solution.py:82
  28.9 1.6 %fusion.151 = (bf16[2048,128]{1,0:T(8,128)(2,1)S(1)}, bf16[2048,128]{1,0:T(8,128)(2,1)S(1)}) fusion(s32[2048]{0:T(1024)S(1)} %bitcast.128, bf16[2048]{0:T(1024)(128)(2,1)S(1)} %get-tuple-element.850, bf16[2048]{0:T(1024)(128)(2,1)S(1)} %get-tuple-element.851), kind=kLoop, calls=%fused_computation.49.clone.1 | loop fusion | flops 786432 | bytes 1064960 | tf_op jit(solution)/shard_map/while/body/eval_jaxpr/jit(_where)/select_n | solution.py:73
  31.1 1.6 %fusion.151 = (bf16[2048,128]{1,0:T(8,128)(2,1)S(1)}, bf16[2048,128]{1,0:T(8,128)(2,1)S(1)}) fusion(s32[2048]{0:T(1024)S(1)} %bitcast.128, bf16[2048]{0:T(1024)(128)(2,1)S(1)} %get-tuple-element.850, bf16[2048]{0:T(1024)(128)(2,1)S(1)} %get-tuple-element.851), kind=kLoop, calls=%fused_computation.49.clone.1 | loop fusion | flops 786432 | bytes 1064960 | tf_op jit(solution)/shard_map/while/body/eval_jaxpr/jit(_where)/select_n | solution.py:73
  33.5 2.8 %while.77 = (s32[]{:T(128)}, f32[2,2048]{1,0:T(2,128)S(1)}, s32[2,2048]{1,0:T(2,128)S(1)}, s32[2,2048]{1,0:T(2,128)S(1)}, bf16[256,256]{1,0:T(8,128)(2,1)S(1)}, /*index=5*/s32[]{:T(128)}, s32[]{:T(128)}) while((s32[]{:T(128)}, f32[2,2048]{1,0:T(2,128)S(1)}, s32[2,2048]{1,0:T(2,128)S(1)}, s32[2,2048]{1,0:T(2,128)S(1)}, ...), condition=%wide.region_7.8_spmd.clone, body=%wide.region_5.7_spmd.clone.sunk | while | flops 270006272 | bytes 4399189 | solution.py:101
  33.6 1.0 fusion.142
  34.9 1.0 fusion.142
  36.3 0.6 all_to_all.55
  36.9 2.5 %all-to-all-start.2 = ((f32[32,1,128]{2,1,0:T(1,128)}), f32[32,1,128]{2,1,0:T(1,128)S(1)}, u32[]{:S(2)}, u32[]{:S(2)}) async-start(f32[32,1,128]{2,1,0:T(1,128)} %all_to_all.55), calls=%async_computation.2 | async-start | bytes 32768 | tf_op jit(solution)/shard_map/all_to_all | solution.py:156
  39.5 7.0 %all-to-all-done.2 = f32[32,1,128]{2,1,0:T(1,128)S(1)} async-done(((f32[32,1,128]{2,1,0:T(1,128)}), f32[32,1,128]{2,1,0:T(1,128)S(1)}, u32[]{:S(2)}, u32[]{:S(2)}) %all-to-all-start.2) | async-done | bytes 16416 | tf_op jit(solution)/shard_map/all_to_all | solution.py:156
  46.5 0.6 reduce.26
  47.7 0.7 all_to_all.57
  48.4 2.5 %all-to-all-start.3 = ((f32[32,1,128]{2,1,0:T(1,128)}), f32[32,1,128]{2,1,0:T(1,128)S(1)}, u32[]{:S(2)}, u32[]{:S(2)}) async-start(f32[32,1,128]{2,1,0:T(1,128)} %bitcast.9), calls=%async_computation.3 | async-start | bytes 32768 | tf_op jit(solution)/shard_map/all_to_all | solution.py:166
  51.1 6.9 %all-to-all-done.3 = f32[32,1,128]{2,1,0:T(1,128)S(1)} async-done(((f32[32,1,128]{2,1,0:T(1,128)}), f32[32,1,128]{2,1,0:T(1,128)S(1)}, u32[]{:S(2)}, u32[]{:S(2)}) %all-to-all-start.3) | async-done | bytes 16416 | tf_op jit(solution)/shard_map/all_to_all | solution.py:166
  58.0 0.6 reduce.27
  58.7 4.5 %while.81 = (s32[]{:T(128)}, f32[256,128]{1,0:T(8,128)S(1)}, s32[2,2048]{1,0:T(2,128)S(1)}, s32[2,2048]{1,0:T(2,128)S(1)}, f32[2,2048]{1,0:T(2,128)S(1)}, /*index=5*/s32[]{:T(128)}, s32[]{:T(128)}) while((s32[]{:T(128)}, f32[256,128]{1,0:T(8,128)S(1)}, s32[2,2048]{1,0:T(2,128)S(1)}, s32[2,2048]{1,0:T(2,128)S(1)}, ...), condition=%wide.region_9.10_spmd.clone, body=%wide.region_8.9_spmd.clone.sunk | while | flops 271949824 | bytes 2973791 | solution.py:82
  58.8 1.6 %fusion.154 = (bf16[2048,128]{1,0:T(8,128)(2,1)S(1)}, bf16[2048,128]{1,0:T(8,128)(2,1)S(1)}) fusion(s32[2048]{0:T(1024)S(1)} %bitcast.129, bf16[2048]{0:T(1024)(128)(2,1)S(1)} %get-tuple-element.861, bf16[2048]{0:T(1024)(128)(2,1)S(1)} %get-tuple-element.862), kind=kLoop, calls=%fused_computation.65.clone.1 | loop fusion | flops 786432 | bytes 1064960 | tf_op jit(solution)/shard_map/while/body/eval_jaxpr/jit(_where)/select_n | solution.py:73
  60.4 0.4 fusion.155
  61.0 1.6 %fusion.154 = (bf16[2048,128]{1,0:T(8,128)(2,1)S(1)}, bf16[2048,128]{1,0:T(8,128)(2,1)S(1)}) fusion(s32[2048]{0:T(1024)S(1)} %bitcast.129, bf16[2048]{0:T(1024)(128)(2,1)S(1)} %get-tuple-element.861, bf16[2048]{0:T(1024)(128)(2,1)S(1)} %get-tuple-element.862), kind=kLoop, calls=%fused_computation.65.clone.1 | loop fusion | flops 786432 | bytes 1064960 | tf_op jit(solution)/shard_map/while/body/eval_jaxpr/jit(_where)/select_n | solution.py:73
  65.5 2.8 %while.78 = (s32[]{:T(128)}, f32[2,2048]{1,0:T(2,128)S(1)}, s32[2,2048]{1,0:T(2,128)S(1)}, s32[2,2048]{1,0:T(2,128)S(1)}, bf16[256,256]{1,0:T(8,128)(2,1)S(1)}, /*index=5*/s32[]{:T(128)}, s32[]{:T(128)}) while((s32[]{:T(128)}, f32[2,2048]{1,0:T(2,128)S(1)}, s32[2,2048]{1,0:T(2,128)S(1)}, s32[2,2048]{1,0:T(2,128)S(1)}, ...), condition=%wide.region_12.13_spmd.clone, body=%wide.region_10.12_spmd.clone.sunk | while | flops 270006272 | bytes 4399189 | solution.py:101
  65.5 1.0 fusion.145
  66.9 1.0 fusion.145
  68.2 0.6 all_to_all.59
  68.9 2.5 %all-to-all-start.4 = ((f32[32,1,128]{2,1,0:T(1,128)}), f32[32,1,128]{2,1,0:T(1,128)S(1)}, u32[]{:S(2)}, u32[]{:S(2)}) async-start(f32[32,1,128]{2,1,0:T(1,128)} %all_to_all.59), calls=%async_computation.4 | async-start | bytes 32768 | tf_op jit(solution)/shard_map/all_to_all | solution.py:156
  71.5 7.0 %all-to-all-done.4 = f32[32,1,128]{2,1,0:T(1,128)S(1)} async-done(((f32[32,1,128]{2,1,0:T(1,128)}), f32[32,1,128]{2,1,0:T(1,128)S(1)}, u32[]{:S(2)}, u32[]{:S(2)}) %all-to-all-start.4) | async-done | bytes 16416 | tf_op jit(solution)/shard_map/all_to_all | solution.py:156
  78.5 0.6 reduce.28
  79.7 0.7 all_to_all.61
  80.4 2.5 %all-to-all-start.5 = ((f32[32,1,128]{2,1,0:T(1,128)}), f32[32,1,128]{2,1,0:T(1,128)S(1)}, u32[]{:S(2)}, u32[]{:S(2)}) async-start(f32[32,1,128]{2,1,0:T(1,128)} %bitcast.13), calls=%async_computation.5 | async-start | bytes 32768 | tf_op jit(solution)/shard_map/all_to_all | solution.py:166
  83.1 6.9 %all-to-all-done.5 = f32[32,1,128]{2,1,0:T(1,128)S(1)} async-done(((f32[32,1,128]{2,1,0:T(1,128)}), f32[32,1,128]{2,1,0:T(1,128)S(1)}, u32[]{:S(2)}, u32[]{:S(2)}) %all-to-all-start.5) | async-done | bytes 16416 | tf_op jit(solution)/shard_map/all_to_all | solution.py:166
  90.0 0.6 reduce.29
  90.6 4.5 %while.82 = (s32[]{:T(128)}, f32[256,128]{1,0:T(8,128)S(1)}, s32[2,2048]{1,0:T(2,128)S(1)}, s32[2,2048]{1,0:T(2,128)S(1)}, f32[2,2048]{1,0:T(2,128)S(1)}, /*index=5*/s32[]{:T(128)}, s32[]{:T(128)}) while((s32[]{:T(128)}, f32[256,128]{1,0:T(8,128)S(1)}, s32[2,2048]{1,0:T(2,128)S(1)}, s32[2,2048]{1,0:T(2,128)S(1)}, ...), condition=%wide.region_14.15_spmd.clone, body=%wide.region_13.14_spmd.clone.sunk | while | flops 271949824 | bytes 2973791 | solution.py:82
  90.7 1.6 %fusion.157 = (bf16[2048,128]{1,0:T(8,128)(2,1)S(1)}, bf16[2048,128]{1,0:T(8,128)(2,1)S(1)}) fusion(s32[2048]{0:T(1024)S(1)} %bitcast.130, bf16[2048]{0:T(1024)(128)(2,1)S(1)} %get-tuple-element.872, bf16[2048]{0:T(1024)(128)(2,1)S(1)} %get-tuple-element.873), kind=kLoop, calls=%fused_computation.81.clone.1 | loop fusion | flops 786432 | bytes 1064960 | tf_op jit(solution)/shard_map/while/body/eval_jaxpr/jit(_where)/select_n | solution.py:73
  92.9 1.6 %fusion.157 = (bf16[2048,128]{1,0:T(8,128)(2,1)S(1)}, bf16[2048,128]{1,0:T(8,128)(2,1)S(1)}) fusion(s32[2048]{0:T(1024)S(1)} %bitcast.130, bf16[2048]{0:T(1024)(128)(2,1)S(1)} %get-tuple-element.872, bf16[2048]{0:T(1024)(128)(2,1)S(1)} %get-tuple-element.873), kind=kLoop, calls=%fused_computation.81.clone.1 | loop fusion | flops 786432 | bytes 1064960 | tf_op jit(solution)/shard_map/while/body/eval_jaxpr/jit(_where)/select_n | solution.py:73
  94.6 0.4 fusion.158
  97.4 2.8 %while.79 = (s32[]{:T(128)}, f32[2,2048]{1,0:T(2,128)S(1)}, s32[2,2048]{1,0:T(2,128)S(1)}, s32[2,2048]{1,0:T(2,128)S(1)}, bf16[256,256]{1,0:T(8,128)(2,1)S(1)}, /*index=5*/s32[]{:T(128)}, s32[]{:T(128)}) while((s32[]{:T(128)}, f32[2,2048]{1,0:T(2,128)S(1)}, s32[2,2048]{1,0:T(2,128)S(1)}, s32[2,2048]{1,0:T(2,128)S(1)}, ...), condition=%wide.region_17.18_spmd.clone, body=%wide.region_15.17_spmd.clone.sunk | while | flops 270006272 | bytes 4399189 | solution.py:101
  97.4 1.0 fusion.148
  98.8 1.0 fusion.148
  100.2 0.6 all_to_all.63
  100.8 2.7 %all-to-all-start.6 = ((f32[32,1,128]{2,1,0:T(1,128)}), f32[32,1,128]{2,1,0:T(1,128)S(1)}, u32[]{:S(2)}, u32[]{:S(2)}) async-start(f32[32,1,128]{2,1,0:T(1,128)} %all_to_all.63), calls=%async_computation.6 | async-start | bytes 32768 | tf_op jit(solution)/shard_map/all_to_all | solution.py:156
  103.6 7.0 %all-to-all-done.6 = f32[32,1,128]{2,1,0:T(1,128)S(1)} async-done(((f32[32,1,128]{2,1,0:T(1,128)}), f32[32,1,128]{2,1,0:T(1,128)S(1)}, u32[]{:S(2)}, u32[]{:S(2)}) %all-to-all-start.6) | async-done | bytes 16416 | tf_op jit(solution)/shard_map/all_to_all | solution.py:156
  110.6 0.6 reduce.30
  111.8 0.7 all_to_all.65
  112.5 2.5 %all-to-all-start.7 = ((f32[32,1,128]{2,1,0:T(1,128)}), f32[32,1,128]{2,1,0:T(1,128)S(1)}, u32[]{:S(2)}, u32[]{:S(2)}) async-start(f32[32,1,128]{2,1,0:T(1,128)} %bitcast.17), calls=%async_computation.7 | async-start | bytes 32768 | tf_op jit(solution)/shard_map/all_to_all | solution.py:166
  115.2 6.9 %all-to-all-done.7 = f32[32,1,128]{2,1,0:T(1,128)S(1)} async-done(((f32[32,1,128]{2,1,0:T(1,128)}), f32[32,1,128]{2,1,0:T(1,128)S(1)}, u32[]{:S(2)}, u32[]{:S(2)}) %all-to-all-start.7) | async-done | bytes 16416 | tf_op jit(solution)/shard_map/all_to_all | solution.py:166
  122.1 0.6 reduce.31
  122.8 4.5 %while.83 = (s32[]{:T(128)}, f32[256,128]{1,0:T(8,128)S(1)}, s32[2,2048]{1,0:T(2,128)S(1)}, s32[2,2048]{1,0:T(2,128)S(1)}, f32[2,2048]{1,0:T(2,128)S(1)}, /*index=5*/s32[]{:T(128)}, s32[]{:T(128)}) while((s32[]{:T(128)}, f32[256,128]{1,0:T(8,128)S(1)}, s32[2,2048]{1,0:T(2,128)S(1)}, s32[2,2048]{1,0:T(2,128)S(1)}, ...), condition=%wide.region_19.20_spmd.clone, body=%wide.region_18.19_spmd.clone.sunk | while | flops 271949824 | bytes 2973791 | solution.py:82
  122.8 1.6 %fusion.160 = (bf16[2048,128]{1,0:T(8,128)(2,1)S(1)}, bf16[2048,128]{1,0:T(8,128)(2,1)S(1)}) fusion(s32[2048]{0:T(1024)S(1)} %bitcast.131, bf16[2048]{0:T(1024)(128)(2,1)S(1)} %get-tuple-element.883, bf16[2048]{0:T(1024)(128)(2,1)S(1)} %get-tuple-element.884), kind=kLoop, calls=%fused_computation.97.clone.1 | loop fusion | flops 786432 | bytes 1064960 | tf_op jit(solution)/shard_map/while/body/eval_jaxpr/jit(_where)/select_n | solution.py:73
  125.1 1.6 %fusion.160 = (bf16[2048,128]{1,0:T(8,128)(2,1)S(1)}, bf16[2048,128]{1,0:T(8,128)(2,1)S(1)}) fusion(s32[2048]{0:T(1024)S(1)} %bitcast.131, bf16[2048]{0:T(1024)(128)(2,1)S(1)} %get-tuple-element.883, bf16[2048]{0:T(1024)(128)(2,1)S(1)} %get-tuple-element.884), kind=kLoop, calls=%fused_computation.97.clone.1 | loop fusion | flops 786432 | bytes 1064960 | tf_op jit(solution)/shard_map/while/body/eval_jaxpr/jit(_where)/select_n | solution.py:73
  126.7 0.4 fusion.161
  130.1 0.8 fusion.73
  (193 shorter events, 15.8 us)
Async XLA Ops:
  3.5 14.4 %all-to-all-start.1 = ((f32[32,1,128]{2,1,0:T(1,128)}), f32[32,1,128]{2,1,0:T(1,128)S(1)}, u32[]{:S(2)}, u32[]{:S(2)}) async-start(f32[32,1,128]{2,1,0:T(1,128)} %bitcast.5), calls=%async_computation.1 | async-start | bytes 32768 | tf_op jit(solution)/shard_map/all_to_all | solution.py:136
  17.9 9.6 %all-to-all-start = ((s32[32,1,128]{2,1,0:T(1,128)}), s32[32,1,128]{2,1,0:T(1,128)S(1)}, u32[]{:S(2)}, u32[]{:S(2)}) async-start(s32[32,1,128]{2,1,0:T(1,128)} %all_to_all.50), calls=%async_computation | async-start | bytes 32768 | tf_op jit(solution)/shard_map/all_to_all | solution.py:135
  28.8 4.5 %copy-start.1 = (f32[2,128,128]{2,1,0:T(8,128)S(1)}, f32[2,128,128]{2,1,0:T(8,128)}, u32[]{:S(2)}) copy-start(f32[2,128,128]{2,1,0:T(8,128)} %param.23) | copy-start | bytes 393220
  33.5 13.9 %copy-start.4 = (f32[16,64]{1,0:T(8,128)S(1)}, f32[16,64]{1,0:T(8,128)}, u32[]{:S(2)}) copy-start(f32[16,64]{1,0:T(8,128)} %param.24) | copy-start | bytes 12292
  36.9 9.6 %all-to-all-start.2 = ((f32[32,1,128]{2,1,0:T(1,128)}), f32[32,1,128]{2,1,0:T(1,128)S(1)}, u32[]{:S(2)}, u32[]{:S(2)}) async-start(f32[32,1,128]{2,1,0:T(1,128)} %all_to_all.55), calls=%async_computation.2 | async-start | bytes 32768 | tf_op jit(solution)/shard_map/all_to_all | solution.py:156
  48.4 9.6 %all-to-all-start.3 = ((f32[32,1,128]{2,1,0:T(1,128)}), f32[32,1,128]{2,1,0:T(1,128)S(1)}, u32[]{:S(2)}, u32[]{:S(2)}) async-start(f32[32,1,128]{2,1,0:T(1,128)} %bitcast.9), calls=%async_computation.3 | async-start | bytes 32768 | tf_op jit(solution)/shard_map/all_to_all | solution.py:166
  68.9 9.6 %all-to-all-start.4 = ((f32[32,1,128]{2,1,0:T(1,128)}), f32[32,1,128]{2,1,0:T(1,128)S(1)}, u32[]{:S(2)}, u32[]{:S(2)}) async-start(f32[32,1,128]{2,1,0:T(1,128)} %all_to_all.59), calls=%async_computation.4 | async-start | bytes 32768 | tf_op jit(solution)/shard_map/all_to_all | solution.py:156
  80.4 9.6 %all-to-all-start.5 = ((f32[32,1,128]{2,1,0:T(1,128)}), f32[32,1,128]{2,1,0:T(1,128)S(1)}, u32[]{:S(2)}, u32[]{:S(2)}) async-start(f32[32,1,128]{2,1,0:T(1,128)} %bitcast.13), calls=%async_computation.5 | async-start | bytes 32768 | tf_op jit(solution)/shard_map/all_to_all | solution.py:166
  100.8 9.8 %all-to-all-start.6 = ((f32[32,1,128]{2,1,0:T(1,128)}), f32[32,1,128]{2,1,0:T(1,128)S(1)}, u32[]{:S(2)}, u32[]{:S(2)}) async-start(f32[32,1,128]{2,1,0:T(1,128)} %all_to_all.63), calls=%async_computation.6 | async-start | bytes 32768 | tf_op jit(solution)/shard_map/all_to_all | solution.py:156
  112.5 9.6 %all-to-all-start.7 = ((f32[32,1,128]{2,1,0:T(1,128)}), f32[32,1,128]{2,1,0:T(1,128)S(1)}, u32[]{:S(2)}, u32[]{:S(2)}) async-start(f32[32,1,128]{2,1,0:T(1,128)} %bitcast.17), calls=%async_computation.7 | async-start | bytes 32768 | tf_op jit(solution)/shard_map/all_to_all | solution.py:166
  128.9 0.9 copy-start.2
  129.1 0.9 copy-start.3
  129.8 1.0 copy-start
where the time goes:
time: 131 us
  waiting for transfers between devices  51 us (39%)
  other arithmetic  30.8 us (24%)
  starting transfers between devices  25.3 us (19%)
  matrix products  11.5 us (9%)
  local copies, waits for them, and re-layouts  10 us (8%)
  between operations  1.54 us (1%)
    all_to_all x3, waiting for transfers between devices, body(): lax.all_to_all(values, ('wide', 'narrow'), split_axis=0, concat_axis=0, t...  21.1 us
    all_to_all x3, waiting for transfers between devices, body(): lax.all_to_all(packed, ('wide', 'narrow'), split_axis=0, concat_axis=0, t...  20.8 us
    select_n x8, other arithmetic, add_block(): jnp.where(col_hot, high_part[:, None], zero_half)  13 us
    all_to_all x3, starting transfers between devices, body(): lax.all_to_all(values, ('wide', 'narrow'), split_axis=0, concat_axis=0, t...  7.81 us
    all_to_all x3, starting transfers between devices, body(): lax.all_to_all(packed, ('wide', 'narrow'), split_axis=0, concat_axis=0, t...  7.63 us
    all_to_all x1, starting transfers between devices, body(): lax.all_to_all(weight_out, ('wide', 'narrow'), split_axis=0, concat_axis=...  7.3 us
    dot_general x6, matrix products, pick_block(): picked = jnp.dot(row_hot, both_parts, preferred_element_type=jnp.float32)  6.25 us
    all_to_all x1, waiting for transfers between devices, body(): lax.all_to_all(outgoing, ('wide', 'narrow'), split_axis=0, concat_axis=0,...  5.79 us
  transfers between devices with their start and end apart: 8, of which 8 were waited for; matrix products, arithmetic and copies ran while one was open for 4% of the time, Pallas kernels for 0%

commit v1 on v0

v1 whole, which is shorter than its diff:
```python
import functools

import jax
import jax.numpy as jnp
from jax import lax
from jax.experimental import pallas as pl
from jax.experimental.pallas import tpu as pltpu
from jax.sharding import PartitionSpec as P

SWEEPS = 3
INNER = 8
LEAKAGE = 0.25
AXES = ("wide", "narrow")
HIGH = lax.Precision.HIGHEST


def pack_kernel(trace_len, cells_per, dest_ref, local_ref, nodes_ref, weight_ref, out_ref, seen_ref):
    owned = nodes_ref.shape[0]
    devices, _, width = out_ref.shape

    def clear(device, carry):
        seen_ref[device] = 0
        return carry

    lax.fori_loop(0, devices, clear, 0, unroll=8)
    lane = lax.broadcasted_iota(jnp.int32, (1, 1, width), 2)
    out_ref[:, 0:2, :] = jnp.zeros((devices, 2, width), jnp.float32)
    out_ref[:, 2:4, :] = jnp.full((devices, 2, width), -1.0, jnp.float32)

    def place(index, carry):
        ends = [dest_ref[0, index], dest_ref[1, index]]
        weights = weight_ref[pl.ds(index, 1), :]
        for side in range(2):
            target = ends[side]
            rank = seen_ref[target]
            seen_ref[target] = rank + 1
            first = local_ref[side, index] * cells_per + 1
            cells = (nodes_ref[index, side : side + 1, :] + first).astype(jnp.float32)
            row = jnp.concatenate([cells, weights], axis=1)
            out_ref[target, pl.ds(rank, 1), :] = row
            out_ref[target, pl.ds(rank + 2, 1), :] = jnp.full(
                (1, width), ends[1 - side].astype(jnp.float32)
            )
        return carry

    lax.fori_loop(0, owned, place, 0, unroll=True)


def face_parts(conduct, grid_size):
    rows, cols = conduct.shape
    row = lax.broadcasted_iota(jnp.int32, (rows, cols), 0) & (grid_size - 1)
    col = lax.broadcasted_iota(jnp.int32, (rows, cols), 1)
    below = jnp.where(row < grid_size - 1, (conduct + pltpu.roll(conduct, rows - 1, 0)) * 0.5, 0.0)
    above = jnp.where(row > 0, (conduct + pltpu.roll(conduct, 1, 0)) * 0.5, 0.0)
    right = jnp.where(col < cols - 1, (conduct + pltpu.roll(conduct, cols - 1, 1)) * 0.5, 0.0)
    left = jnp.where(col > 0, (conduct + pltpu.roll(conduct, 1, 1)) * 0.5, 0.0)
    return below, above, right, left


def shifted(field):
    rows, cols = field.shape
    return (
        pltpu.roll(field, rows - 1, 0),
        pltpu.roll(field, 1, 0),
        pltpu.roll(field, cols - 1, 1),
        pltpu.roll(field, 1, 1),
    )


def split_pair(values):
    high_part = values.astype(jnp.bfloat16)
    low_part = (values - high_part.astype(jnp.float32)).astype(jnp.bfloat16)
    return high_part, low_part


def scatter(row_hot_ref, col_hot_ref, spread_ref, value_of, devices, width, cols):
    for device in range(devices):
        lanes = slice(device * width, (device + 1) * width)
        high_part, low_part = split_pair(value_of(device))
        hot = col_hot_ref[:, lanes]
        spread_ref[0:cols, lanes] = hot * high_part
        spread_ref[cols : 2 * cols, lanes] = hot * low_part
    both = lax.dot_general(
        row_hot_ref[...], spread_ref[...], (((1,), (1,)), ((), ())), preferred_element_type=jnp.float32
    )
    return both[:, :cols] + both[:, cols:]


def gather(row_hot_ref, col_ref, field, out_ref, devices, width):
    cols = field.shape[1]
    high_part, low_part = split_pair(field.T)
    both = jnp.concatenate([high_part, low_part], axis=0)
    group = 2 if devices % 2 == 0 else 1
    col_ids = lax.broadcasted_iota(jnp.int32, (cols, width), 0)
    for start in range(0, devices, group):
        picked = jnp.dot(
            both,
            row_hot_ref[:, start * width : (start + group) * width],
            preferred_element_type=jnp.float32,
        )
        picked = picked[:cols] + picked[cols:]
        for offset in range(group):
            device = start + offset
            mine = picked[:, offset * width : (offset + 1) * width]
            hit = col_ids == col_ref[device : device + 1, :]
            out_ref[device] = jnp.sum(jnp.where(hit, mine, 0.0), axis=0, keepdims=True)


def first_kernel(
    grid_size, message_ref, aperture_ref, source_ref,
    values_ref, row_hot_ref, col_hot_ref, col_ref, weight_ref, parts_ref, spread_ref,
):
    devices, _, width = message_ref.shape
    trace_len = width // 2
    rows, cols = aperture_ref.shape
    slots = [message_ref[:, rank, :] for rank in range(2)]
    partners = [message_ref[:, 2 + rank, :] for rank in range(2)]
    owner = lax.broadcasted_iota(jnp.int32, (devices, width), 0)
    lane = lax.broadcasted_iota(jnp.int32, (devices, width), 1)
    along = [
        jnp.sum(jnp.where(owner == lane, partners[rank], 0.0), axis=0, keepdims=True)
        for rank in range(2)
    ]
    place_id = owner.astype(jnp.float32)
    ordered = [jnp.zeros((devices, width), jnp.float32) for _ in range(2)]
    for rank in range(2):
        same = [(partners[other] == along[rank]) for other in range(2)]
        before = [owner < lane, owner < lane if rank == 0 else owner <= lane]
        earlier = jnp.where(same[1] & (owner < lane), 1.0, 0.0)
        earlier = earlier + jnp.where(
            same[0] & ((owner < lane) if rank == 0 else (owner <= lane)), 1.0, 0.0
        )
        position = jnp.sum(earlier, axis=0, keepdims=True)
        position = jnp.where(lane[0:1] < devices, position, -1.0)
        for spot in range(2):
            pick = jnp.where((place_id == along[rank]) & (position == float(spot)), 1.0, 0.0)
            ordered[spot] = ordered[spot] + jnp.dot(
                pick[:, :devices], slots[rank], precision=HIGH, preferred_element_type=jnp.float32
            )
    front = lane < trace_len
    cell = jnp.where(front, ordered[0], pltpu.roll(ordered[1], trace_len, 1)).astype(jnp.int32) - 1
    weight_ref[...] = jnp.where(front, pltpu.roll(ordered[0], trace_len, 1), ordered[1])
    row = cell >> (grid_size.bit_length() - 1)
    col = cell & (grid_size - 1)
    col_ref[...] = col
    row_ids = lax.broadcasted_iota(jnp.int32, (rows, width), 0)
    col_ids = lax.broadcasted_iota(jnp.int32, (cols, width), 0)
    for device in range(devices):
        lanes = slice(device * width, (device + 1) * width)
        row_hot_ref[:, lanes] = jnp.where(row_ids == row[device : device + 1], 1.0, 0.0).astype(jnp.bfloat16)
        col_hot_ref[:, lanes] = jnp.where(col_ids == col[device : device + 1], 1.0, 0.0).astype(jnp.bfloat16)
    trace_sum = scatter(
        row_hot_ref, col_hot_ref, spread_ref, lambda device: weight_ref[device : device + 1, :], devices, width, cols
    )
    aperture = aperture_ref[...]
    faces = face_parts(aperture * aperture * aperture / 12.0, grid_size)
    inv_diag = 1.0 / (LEAKAGE + (faces[0] + faces[1] + faces[2] + faces[3]) + trace_sum)
    for index in range(4):
        parts_ref[index] = faces[index] * inv_diag
    parts_ref[4] = inv_diag
    adjoint = source_ref[...] * inv_diag
    parts_ref[5] = adjoint
    gather(row_hot_ref, col_ref, adjoint, values_ref, devices, width)


def relax(arrived_ref, row_hot_ref, col_hot_ref, weight_ref, parts_ref, start, source_ref, spread_ref):
    devices, _, width = arrived_ref.shape
    cols = source_ref.shape[1]
    coupling = scatter(
        row_hot_ref, col_hot_ref, spread_ref,
        lambda device: weight_ref[device : device + 1, :] * arrived_ref[device], devices, width, cols,
    )
    forcing = (source_ref[...] + coupling) * parts_ref[4]
    adjoint = start
    for _ in range(INNER):
        below, above, right, left = shifted(adjoint)
        adjoint = (
            forcing + (parts_ref[0] * below + parts_ref[1] * above)
            + (parts_ref[2] * right + parts_ref[3] * left)
        )
    return adjoint


def sweep_kernel(
    arrived_ref, row_hot_ref, col_hot_ref, col_ref, weight_ref, parts_ref, start_ref, source_ref,
    values_ref, adjoint_ref, spread_ref,
):
    devices, _, width = arrived_ref.shape
    adjoint = relax(
        arrived_ref, row_hot_ref, col_hot_ref, weight_ref, parts_ref, start_ref[...], source_ref, spread_ref
    )
    adjoint_ref[...] = adjoint
    gather(row_hot_ref, col_ref, adjoint, values_ref, devices, width)


def last_kernel(
    grid_size, arrived_ref, row_hot_ref, col_hot_ref, weight_ref, parts_ref, start_ref, source_ref,
    aperture_ref, pressure_ref, gradient_ref, adjoint_ref, spread_ref,
):
    adjoint = relax(
        arrived_ref, row_hot_ref, col_hot_ref, weight_ref, parts_ref, start_ref[...], source_ref, spread_ref
    )
    adjoint_ref[...] = adjoint
    pressure = pressure_ref[...]
    rows, cols = adjoint.shape
    row = lax.broadcasted_iota(jnp.int32, (rows, cols), 0) & (grid_size - 1)
    col = lax.broadcasted_iota(jnp.int32, (rows, cols), 1)
    inside = (row < grid_size - 1, row > 0, col < cols - 1, col > 0)
    total = jnp.zeros((rows, cols), jnp.float32)
    for keep, near_pressure, near_adjoint in zip(inside, shifted(pressure), shifted(adjoint), strict=True):
        total = total + jnp.where(keep, (pressure - near_pressure) * (adjoint - near_adjoint), 0.0)
    aperture = aperture_ref[...]
    gradient_ref[...] = -(aperture * aperture / 8.0) * total


def body(aperture, pressure, adj_source, trace_weight, end_device, end_local, trace_nodes):
    frac_count, grid_size, _ = aperture.shape
    owned_count, trace_len = trace_weight.shape
    device_count = lax.axis_size(AXES)
    rows, cols, width = frac_count * grid_size, grid_size, 2 * trace_len
    nodes = device_count * width
    in_vmem = pl.BlockSpec(memory_space=pltpu.VMEM)
    in_smem = pl.BlockSpec(memory_space=pltpu.SMEM)
    params = pltpu.CompilerParams(vmem_limit_bytes=(8 << 20) + nodes * 2560)
    spread = pltpu.VMEM((2 * cols, nodes), jnp.bfloat16)

    def flat(field):
        return field.reshape(rows, cols)

    def vmem(*arrays):
        return [pltpu.with_memory_space_constraint(array, pltpu.VMEM) for array in arrays]

    def exchange(values):
        return lax.all_to_all(values, AXES, split_axis=0, concat_axis=0, tiled=True)

    message = pl.pallas_call(
        functools.partial(pack_kernel, trace_len, grid_size * grid_size),
        out_shape=pltpu.VMEM((device_count, 4, width), jnp.float32),
        in_specs=[in_smem, in_smem, in_vmem, in_vmem],
        out_specs=in_vmem,
        scratch_shapes=[pltpu.SMEM((device_count,), jnp.int32)],
        compiler_params=params,
        name="pack_ends",
    )(end_device.T, end_local.T, trace_nodes, trace_weight)
    values_shape = pltpu.VMEM((device_count, 1, width), jnp.float32)
    field_shape = pltpu.VMEM((rows, cols), jnp.float32)
    values, row_hot, col_hot, col, weight, parts = pl.pallas_call(
        functools.partial(first_kernel, grid_size),
        out_shape=[
            values_shape,
            pltpu.VMEM((rows, nodes), jnp.bfloat16),
            pltpu.VMEM((cols, nodes), jnp.bfloat16),
            pltpu.VMEM((device_count, width), jnp.int32),
            pltpu.VMEM((device_count, width), jnp.float32),
            pltpu.VMEM((6, rows, cols), jnp.float32),
        ],
        in_specs=[in_vmem] * 3,
        out_specs=[in_vmem] * 6,
        scratch_shapes=[spread],
        compiler_params=params,
        name="first_values",
    )(*vmem(exchange(message)), flat(aperture), flat(adj_source))
    adjoint = parts[5]
    for _ in range(SWEEPS - 1):
        values, adjoint = pl.pallas_call(
            sweep_kernel,
            out_shape=[values_shape, field_shape],
            in_specs=[in_vmem] * 8,
            out_specs=[in_vmem] * 2,
            scratch_shapes=[spread],
            compiler_params=params,
            name="sweep",
        )(*vmem(exchange(values), row_hot, col_hot, col, weight, parts, adjoint), flat(adj_source))
    gradient, adjoint = pl.pallas_call(
        functools.partial(last_kernel, grid_size),
        out_shape=[jax.ShapeDtypeStruct((rows, cols), jnp.float32)] * 2,
        in_specs=[in_vmem] * 9,
        out_specs=[in_vmem] * 2,
        scratch_shapes=[spread],
        compiler_params=params,
        name="last_sweep",
    )(
        *vmem(exchange(values), row_hot, col_hot, weight, parts, adjoint),
        flat(adj_source), flat(aperture), flat(pressure),
    )
    return gradient.reshape(aperture.shape), adjoint.reshape(aperture.shape)


def solution(mesh):
    fields, pairs = P(AXES, None, None), P(AXES, None)
    return jax.shard_map(
        body,
        mesh=mesh,
        in_specs=(fields, fields, fields, pairs, pairs, pairs, fields),
        out_specs=(fields, fields),
        check_vma=False,
    )
```

time: 131 us -> 63.4 us (0.48)
  waiting for transfers between devices: 51 us -> 6.16 us
  blocking collectives: 0 us -> 32.2 us
  other arithmetic: 30.8 us -> 0 us
  starting transfers between devices: 25.3 us -> 2.54 us
  Pallas kernels: 0 us -> 12.9 us
  matrix products: 11.5 us -> 0 us
  local copies, waits for them, and re-layouts: 10 us -> 8.43 us
    all_to_all x8 -> x1, waiting for transfers between devices: 51 us -> 6.16 us  [exchange(): return lax.all_to_all(values, AXES, split_axis=0, concat_axis=0, tiled=True)]
    all_to_all x0 -> x3, blocking collectives: none -> 32.2 us  [exchange(): return lax.all_to_all(values, AXES, split_axis=0, concat_axis=0, tiled=True)]
    all_to_all x8 -> x1, starting transfers between devices: 25.3 us -> 2.54 us  [exchange(): return lax.all_to_all(values, AXES, split_axis=0, concat_axis=0, tiled=True)]
    select_n x14 -> x0, other arithmetic: 13.1 us -> none  [the longest x8 13 us: add_block(): jnp.where(col_hot, high_part[:, None], zero_half)]
    pallas_call x0 -> x5, Pallas kernels: none -> 12.9 us  [the longest x2 6.09 us: body(): pl.pallas_call(sweep_kernel, out_shape=[values_shape, field_shape], in_sp...]
    dot_general x21 -> x0, matrix products: 11.5 us -> none  [the longest x6 6.25 us: pick_block(): picked = jnp.dot(row_hot, both_parts, preferred_element_type=jnp.float32)]
    mul x82 -> x0, other arithmetic: 8.67 us -> none  [the longest x24 3.16 us: neighbours(): total = total + jnp.pad(face_y * field[:, :, 1:], ((0, 0), (0, 0), (0, 1)))]
    all_to_all x11 -> x0, local copies, waits for them, and re-layouts: 6.35 us -> none  [the longest x3 2.04 us: body(): lax.all_to_all(packed, ('wide', 'narrow'), split_axis=0, concat_axis=0, t...]
  transfers between devices with their start and end apart: 8 -> 1, of which waited for: 8 -> 1; matrix products, arithmetic and copies ran while one was open for 4% -> 1% of each run, Pallas kernels for 0% -> 0%
where the time goes in v1:
time: 63.4 us; the launch traced here: 62.9 us
  blocking collectives  32.2 us (51%)
  Pallas kernels  12.9 us (20%)
  local copies, waits for them, and re-layouts  8.43 us (13%)
  waiting for transfers between devices  6.16 us (10%)
  starting transfers between devices  2.54 us (4%)
  between operations  0.69 us (1%)
    all_to_all x3, blocking collectives, exchange(): return lax.all_to_all(values, AXES, split_axis=0, concat_axis=0, tiled=True)  32.2 us
    unnamed x24, local copies, waits for them, and re-layouts  7.52 us
    all_to_all x1, waiting for transfers between devices, exchange(): return lax.all_to_all(values, AXES, split_axis=0, concat_axis=0, tiled=True)  6.16 us
    pallas_call x2, Pallas kernels, body(): pl.pallas_call(sweep_kernel, out_shape=[values_shape, field_shape], in_sp...  6.09 us
    pallas_call x1, Pallas kernels, body(): pl.pallas_call(functools.partial(first_kernel, grid_size), out_shape=[val...  3.94 us
    all_to_all x1, starting transfers between devices, exchange(): return lax.all_to_all(values, AXES, split_axis=0, concat_axis=0, tiled=True)  2.54 us
    pallas_call x1, Pallas kernels, body(): pl.pallas_call(functools.partial(last_kernel, grid_size), out_shape=[jax....  2.11 us
  transfers between devices with their start and end apart: 1, of which 1 were waited for; matrix products, arithmetic and copies ran while one was open for 1% of the time, Pallas kernels for 0%

profile of v1, /device:TPU:0, one launch (start us, length us, event | category | flops | bytes accessed | tf_op | source)
XLA Modules:
  0.0 62.9 jit_solution(480792768069068552)
XLA Ops:
  0.6 0.0 copy-start.8
  0.6 0.7 %copy-done.8 = s32[16,2,64]{2,1,0:T(2,128)S(1)} copy-done((s32[16,2,64]{2,1,0:T(2,128)S(1)}, s32[16,2,64]{2,1,0:T(2,128)}, u32[]{:S(2)}) %copy-start.8) | copy-done | bytes 8216
  1.3 0.0 copy-start.9
  1.4 0.7 %copy-done.9 = f32[16,64]{1,0:T(8,128)S(1)} copy-done((f32[16,64]{1,0:T(8,128)S(1)}, f32[16,64]{1,0:T(8,128)}, u32[]{:S(2)}) %copy-start.9) | copy-done | bytes 4120
  2.0 0.0 copy-start.10
  2.0 0.7 %copy-done.10 = s32[16,2]{0,1:T(2,128)S(1)} copy-done((s32[16,2]{0,1:T(2,128)S(1)}, s32[16,2]{0,1:T(2,128)}, u32[]{:S(2)}) %copy-start.10) | copy-done | bytes 152
  2.7 0.0 copy-start.11
  2.7 0.7 %copy-done.11 = s32[16,2]{0,1:T(2,128)S(1)} copy-done((s32[16,2]{0,1:T(2,128)S(1)}, s32[16,2]{0,1:T(2,128)}, u32[]{:S(2)}) %copy-start.11) | copy-done | bytes 152
  3.4 0.8 %pack_ends.1 = f32[32,4,128]{2,1,0:T(4,128)S(1)} custom-call(s32[2,16]{1,0:T(2,128)S(1)} %bitcast.16, s32[2,16]{1,0:T(2,128)S(1)} %bitcast.17, s32[16,2,64]{2,1,0:T(2,128)S(1)} %copy-done.8, f32[16,64]{1,0:T(8,128)S(1)} %copy-done.9), custom_call_target="tpu_custom_call" | custom-call | tf_op jit(solution)/shard_map/pack_ends/pallas_call | solution.py:236
  4.2 14.5 %all_to_all.20.message_ref = f32[32,4,128]{2,1,0:T(4,128)S(1)} all-to-all(f32[32,4,128]{2,1,0:T(4,128)S(1)} %pack_ends.1), channel_id=1, replica_groups=mesh['wide'=8,'narrow'=4] {'wide','narrow'}, dimensions={0} | all-to-all | bytes 131072 | tf_op jit(solution)/shard_map/all_to_all | solution.py:234
  18.7 0.0 copy-start.2
  18.7 0.9 %copy-done.2 = f32[2,128,128]{2,1,0:T(8,128)S(1)} copy-done((f32[2,128,128]{2,1,0:T(8,128)S(1)}, f32[2,128,128]{2,1,0:T(8,128)}, u32[]{:S(2)}) %copy-start.2) | copy-done | bytes 131096
  19.6 0.0 copy-start.5
  19.6 0.9 %copy-done.5 = f32[2,128,128]{2,1,0:T(8,128)S(1)} copy-done((f32[2,128,128]{2,1,0:T(8,128)S(1)}, f32[2,128,128]{2,1,0:T(8,128)}, u32[]{:S(2)}) %copy-start.5) | copy-done | bytes 131096
  20.5 3.9 %first_values.1 = (f32[32,1,128]{2,1,0:T(1,128)}, bf16[256,4096]{1,0:T(8,128)(2,1)S(1)}, bf16[128,4096]{1,0:T(8,128)(2,1)S(1)}, s32[32,128]{1,0:T(8,128)S(1)}, f...) custom-call(f32[32,4,128]{2,1,0:T(4,128)S(1)} %all_to_all.20.message_ref, f32[256,128]{1,0:T(8,128)S(1)} %bitcast.13, ...), custom_call_target="tpu_custom_call" | custom-call | tf_op jit(solution)/shard_map/first_values/pallas_call | solution.py:247
  24.4 0.0 copy-start
  24.4 0.9 %copy-done = f32[6,256,128]{2,1,0:T(8,128)} copy-done((f32[6,256,128]{2,1,0:T(8,128)}, f32[6,256,128]{2,1,0:T(8,128)S(1)}, u32[]{:S(2)}) %copy-start) | copy-done | bytes 786456
  25.3 2.5 %all-to-all-start.1 = ((f32[32,1,128]{2,1,0:T(1,128)}), f32[32,1,128]{2,1,0:T(1,128)S(1)}, u32[]{:S(2)}, u32[]{:S(2)}) async-start(f32[32,1,128]{2,1,0:T(1,128)} %get-tuple-element.14), calls=%async_computation.1 | async-start | bytes 32768 | tf_op jit(solution)/shard_map/all_to_all | solution.py:234
  27.9 0.9 %slice_bitcast_fusion.start_ref = f32[256,128]{1,0:T(8,128)S(1)} fusion(f32[6,256,128]{2,1,0:T(8,128)} %copy-done), kind=kLoop, calls=%fused_computation | loop fusion | bytes 262144 | tf_op jit(solution)/shard_map/squeeze | solution.py:263
  28.8 6.2 %all-to-all-done.1.arrived_ref = f32[32,1,128]{2,1,0:T(1,128)S(1)} async-done(((f32[32,1,128]{2,1,0:T(1,128)}), f32[32,1,128]{2,1,0:T(1,128)S(1)}, u32[]{:S(2)}, u32[]{:S(2)}) %all-to-all-start.1) | async-done | bytes 16416 | tf_op jit(solution)/shard_map/all_to_all | solution.py:234
  35.0 0.0 copy-start.1
  35.0 1.1 %copy-done.1 = f32[6,256,128]{2,1,0:T(8,128)S(1)} copy-done((f32[6,256,128]{2,1,0:T(8,128)S(1)}, f32[6,256,128]{2,1,0:T(8,128)}, u32[]{:S(2)}) %copy-start.1) | copy-done | bytes 786456
  36.1 0.0 copy-start.3
  36.1 0.9 %copy-done.3 = f32[2,128,128]{2,1,0:T(8,128)S(1)} copy-done((f32[2,128,128]{2,1,0:T(8,128)S(1)}, f32[2,128,128]{2,1,0:T(8,128)}, u32[]{:S(2)}) %copy-start.3) | copy-done | bytes 131096
  37.0 3.0 %sweep.2 = (f32[32,1,128]{2,1,0:T(1,128)S(1)}, f32[256,128]{1,0:T(8,128)S(1)}) custom-call(f32[32,1,128]{2,1,0:T(1,128)S(1)} %all-to-all-done.1.arrived_ref, bf16[256,4096]{1,0:T(8,128)(2,1)S(1)} %get-tuple-element.15.row_hot_ref, bf16[128,4096]{1,0:T(8,128)(2,1)S(1)} %get-tuple-element.16.col_hot_ref, s32[32,128]{1,0:T(8,128)S(1)} %get-tuple-element.17.col_ref, ...), custom_call_target="tpu_custom_call" | custom-call | tf_op jit(solution)/shard_map/sweep/pallas_call | solution.py:265
  40.1 8.8 %all_to_all.21.arrived_ref = f32[32,1,128]{2,1,0:T(1,128)S(1)} all-to-all(f32[32,1,128]{2,1,0:T(1,128)S(1)} %get-tuple-element.20), channel_id=1, replica_groups=mesh['wide'=8,'narrow'=4] {'wide','narrow'}, dimensions={0} | all-to-all | bytes 32768 | tf_op jit(solution)/shard_map/all_to_all | solution.py:234
  48.9 0.0 copy-start.4
  48.9 0.0 copy-start.6
  48.9 0.0 copy-start.7
  48.9 3.0 %sweep.3 = (f32[32,1,128]{2,1,0:T(1,128)S(1)}, f32[256,128]{1,0:T(8,128)S(1)}) custom-call(f32[32,1,128]{2,1,0:T(1,128)S(1)} %all_to_all.21.arrived_ref, bf16[256,4096]{1,0:T(8,128)(2,1)S(1)} %get-tuple-element.15.row_hot_ref, bf16[128,4096]{1,0:T(8,128)(2,1)S(1)} %get-tuple-element.16.col_hot_ref, s32[32,128]{1,0:T(8,128)S(1)} %get-tuple-element.17.col_ref, ...), custom_call_target="tpu_custom_call" | custom-call | tf_op jit(solution)/shard_map/sweep/pallas_call | solution.py:265
  52.0 8.8 %all_to_all.22.arrived_ref = f32[32,1,128]{2,1,0:T(1,128)S(1)} all-to-all(f32[32,1,128]{2,1,0:T(1,128)S(1)} %get-tuple-element.22), channel_id=1, replica_groups=mesh['wide'=8,'narrow'=4] {'wide','narrow'}, dimensions={0} | all-to-all | bytes 32768 | tf_op jit(solution)/shard_map/all_to_all | solution.py:234
  60.8 0.0 copy-done.4
  60.8 0.0 copy-done.6
  60.8 0.0 copy-done.7
  60.8 2.1 %last_sweep.1 = (f32[256,128]{1,0:T(8,128)}, f32[256,128]{1,0:T(8,128)}) custom-call(f32[32,1,128]{2,1,0:T(1,128)S(1)} %all_to_all.22.arrived_ref, bf16[256,4096]{1,0:T(8,128)(2,1)S(1)} %get-tuple-element.15.row_hot_ref, bf16[128,4096]{1,0:T(8,128)(2,1)S(1)} %get-tuple-element.16.col_hot_ref, f32[32,128]{1,0:T(8,128)S(1)} %get-tuple-element.18.weight_ref, ...), custom_call_target="tpu_custom_call" | custom-call | tf_op jit(solution)/shard_map/last_sweep/pallas_call | solution.py:274
Async XLA Ops:
  0.6 0.7 %copy-start.8 = (s32[16,2,64]{2,1,0:T(2,128)S(1)}, s32[16,2,64]{2,1,0:T(2,128)}, u32[]{:S(2)}) copy-start(s32[16,2,64]{2,1,0:T(2,128)} %nodes_ref.1) | copy-start | bytes 24580
  1.3 0.7 %copy-start.9 = (f32[16,64]{1,0:T(8,128)S(1)}, f32[16,64]{1,0:T(8,128)}, u32[]{:S(2)}) copy-start(f32[16,64]{1,0:T(8,128)} %weight_ref.1) | copy-start | bytes 12292
  2.0 0.7 %copy-start.10 = (s32[16,2]{0,1:T(2,128)S(1)}, s32[16,2]{0,1:T(2,128)}, u32[]{:S(2)}) copy-start(s32[16,2]{0,1:T(2,128)} %param.11) | copy-start | bytes 388
  2.7 0.7 %copy-start.11 = (s32[16,2]{0,1:T(2,128)S(1)}, s32[16,2]{0,1:T(2,128)}, u32[]{:S(2)}) copy-start(s32[16,2]{0,1:T(2,128)} %param.12) | copy-start | bytes 388
  18.7 0.9 %copy-start.2 = (f32[2,128,128]{2,1,0:T(8,128)S(1)}, f32[2,128,128]{2,1,0:T(8,128)}, u32[]{:S(2)}) copy-start(f32[2,128,128]{2,1,0:T(8,128)} %param.9) | copy-start | bytes 393220
  19.6 0.9 %copy-start.5 = (f32[2,128,128]{2,1,0:T(8,128)S(1)}, f32[2,128,128]{2,1,0:T(8,128)}, u32[]{:S(2)}) copy-start(f32[2,128,128]{2,1,0:T(8,128)} %param.7) | copy-start | bytes 393220
  24.4 0.9 %copy-start = (f32[6,256,128]{2,1,0:T(8,128)}, f32[6,256,128]{2,1,0:T(8,128)S(1)}, u32[]{:S(2)}) copy-start(f32[6,256,128]{2,1,0:T(8,128)S(1)} %get-tuple-element.19.parts_ref) | copy-start | bytes 2359300
  25.3 9.6 %all-to-all-start.1 = ((f32[32,1,128]{2,1,0:T(1,128)}), f32[32,1,128]{2,1,0:T(1,128)S(1)}, u32[]{:S(2)}, u32[]{:S(2)}) async-start(f32[32,1,128]{2,1,0:T(1,128)} %get-tuple-element.14), calls=%async_computation.1 | async-start | bytes 32768 | tf_op jit(solution)/shard_map/all_to_all | solution.py:234
  35.0 1.1 %copy-start.1 = (f32[6,256,128]{2,1,0:T(8,128)S(1)}, f32[6,256,128]{2,1,0:T(8,128)}, u32[]{:S(2)}) copy-start(f32[6,256,128]{2,1,0:T(8,128)} %copy-done) | copy-start | bytes 2359300
  36.1 0.9 %copy-start.3 = (f32[2,128,128]{2,1,0:T(8,128)S(1)}, f32[2,128,128]{2,1,0:T(8,128)}, u32[]{:S(2)}) copy-start(f32[2,128,128]{2,1,0:T(8,128)} %param.9) | copy-start | bytes 393220
  48.9 11.9 %copy-start.4 = (f32[2,128,128]{2,1,0:T(8,128)S(1)}, f32[2,128,128]{2,1,0:T(8,128)}, u32[]{:S(2)}) copy-start(f32[2,128,128]{2,1,0:T(8,128)} %param.9) | copy-start | bytes 393220
  48.9 11.9 %copy-start.6 = (f32[2,128,128]{2,1,0:T(8,128)S(1)}, f32[2,128,128]{2,1,0:T(8,128)}, u32[]{:S(2)}) copy-start(f32[2,128,128]{2,1,0:T(8,128)} %param.7) | copy-start | bytes 393220
  48.9 11.9 %copy-start.7 = (f32[2,128,128]{2,1,0:T(8,128)S(1)}, f32[2,128,128]{2,1,0:T(8,128)}, u32[]{:S(2)}) copy-start(f32[2,128,128]{2,1,0:T(8,128)} %param.8) | copy-start | bytes 393220

commit v2 on v1

--- a/solution.py
+++ b/solution.py
@@ -14,18 +14,37 @@
 HIGH = lax.Precision.HIGHEST
 
 
-def pack_kernel(trace_len, cells_per, dest_ref, local_ref, nodes_ref, weight_ref, out_ref, seen_ref):
+def pack_kernel(
+    cells_per, dest_hbm, local_hbm, nodes_hbm, weight_hbm, aperture_hbm, source_hbm, pressure_hbm,
+    out_ref, aperture_ref, source_ref, pressure_ref,
+    dest_ref, local_ref, nodes_ref, weight_ref, seen_ref, small_sems, large_sems,
+):
     owned = nodes_ref.shape[0]
     devices, _, width = out_ref.shape
+    small = [
+        pltpu.make_async_copy(source, target, small_sems.at[index])
+        for index, (source, target) in enumerate(
+            ((dest_hbm, dest_ref), (local_hbm, local_ref), (nodes_hbm, nodes_ref), (weight_hbm, weight_ref))
+        )
+    ]
+    large = [
+        pltpu.make_async_copy(source, target, large_sems.at[index])
+        for index, (source, target) in enumerate(
+            ((aperture_hbm, aperture_ref), (source_hbm, source_ref), (pressure_hbm, pressure_ref))
+        )
+    ]
+    for copy in small + large:
+        copy.start()
 
     def clear(device, carry):
         seen_ref[device] = 0
         return carry
 
     lax.fori_loop(0, devices, clear, 0, unroll=8)
-    lane = lax.broadcasted_iota(jnp.int32, (1, 1, width), 2)
     out_ref[:, 0:2, :] = jnp.zeros((devices, 2, width), jnp.float32)
     out_ref[:, 2:4, :] = jnp.full((devices, 2, width), -1.0, jnp.float32)
+    for copy in small:
+        copy.wait()
 
     def place(index, carry):
         ends = [dest_ref[0, index], dest_ref[1, index]]
@@ -36,14 +55,15 @@
             seen_ref[target] = rank + 1
             first = local_ref[side, index] * cells_per + 1
             cells = (nodes_ref[index, side : side + 1, :] + first).astype(jnp.float32)
-            row = jnp.concatenate([cells, weights], axis=1)
-            out_ref[target, pl.ds(rank, 1), :] = row
+            out_ref[target, pl.ds(rank, 1), :] = jnp.concatenate([cells, weights], axis=1)
             out_ref[target, pl.ds(rank + 2, 1), :] = jnp.full(
                 (1, width), ends[1 - side].astype(jnp.float32)
             )
         return carry
 
     lax.fori_loop(0, owned, place, 0, unroll=True)
+    for copy in large:
+        copy.wait()
 
 
 def face_parts(conduct, grid_size):
@@ -108,7 +128,7 @@
 
 def first_kernel(
     grid_size, message_ref, aperture_ref, source_ref,
-    values_ref, row_hot_ref, col_hot_ref, col_ref, weight_ref, parts_ref, spread_ref,
+    values_ref, row_hot_ref, col_hot_ref, col_ref, weight_ref, parts_ref, adjoint_ref, spread_ref,
 ):
     devices, _, width = message_ref.shape
     trace_len = width // 2
@@ -125,7 +145,6 @@
     ordered = [jnp.zeros((devices, width), jnp.float32) for _ in range(2)]
     for rank in range(2):
         same = [(partners[other] == along[rank]) for other in range(2)]
-        before = [owner < lane, owner < lane if rank == 0 else owner <= lane]
         earlier = jnp.where(same[1] & (owner < lane), 1.0, 0.0)
         earlier = earlier + jnp.where(
             same[0] & ((owner < lane) if rank == 0 else (owner <= lane)), 1.0, 0.0
@@ -159,7 +178,7 @@
         parts_ref[index] = faces[index] * inv_diag
     parts_ref[4] = inv_diag
     adjoint = source_ref[...] * inv_diag
-    parts_ref[5] = adjoint
+    adjoint_ref[...] = adjoint
     gather(row_hot_ref, col_ref, adjoint, values_ref, devices, width)
 
 
@@ -233,18 +252,30 @@
     def exchange(values):
         return lax.all_to_all(values, AXES, split_axis=0, concat_axis=0, tiled=True)
 
-    message = pl.pallas_call(
-        functools.partial(pack_kernel, trace_len, grid_size * grid_size),
-        out_shape=pltpu.VMEM((device_count, 4, width), jnp.float32),
-        in_specs=[in_smem, in_smem, in_vmem, in_vmem],
-        out_specs=in_vmem,
-        scratch_shapes=[pltpu.SMEM((device_count,), jnp.int32)],
+    field_shape = pltpu.VMEM((rows, cols), jnp.float32)
+    in_hbm = pl.BlockSpec(memory_space=pltpu.HBM)
+    arguments = (
+        end_device.T, end_local.T, trace_nodes, trace_weight, flat(aperture), flat(adj_source), flat(pressure)
+    )
+    message, aperture_here, source_here, pressure_here = pl.pallas_call(
+        functools.partial(pack_kernel, grid_size * grid_size),
+        out_shape=[pltpu.VMEM((device_count, 4, width), jnp.float32)] + [field_shape] * 3,
+        in_specs=[in_hbm] * 7,
+        out_specs=[in_vmem] * 4,
+        scratch_shapes=[
+            pltpu.SMEM((2, owned_count), jnp.int32),
+            pltpu.SMEM((2, owned_count), jnp.int32),
+            pltpu.VMEM(trace_nodes.shape, jnp.int32),
+            pltpu.VMEM(trace_weight.shape, jnp.float32),
+            pltpu.SMEM((device_count,), jnp.int32),
+            pltpu.SemaphoreType.DMA((4,)),
+            pltpu.SemaphoreType.DMA((3,)),
+        ],
         compiler_params=params,
         name="pack_ends",
-    )(end_device.T, end_local.T, trace_nodes, trace_weight)
+    )(*[pltpu.with_memory_space_constraint(array, pltpu.HBM) for array in arguments])
     values_shape = pltpu.VMEM((device_count, 1, width), jnp.float32)
-    field_shape = pltpu.VMEM((rows, cols), jnp.float32)
-    values, row_hot, col_hot, col, weight, parts = pl.pallas_call(
+    values, row_hot, col_hot, col, weight, parts, adjoint = pl.pallas_call(
         functools.partial(first_kernel, grid_size),
         out_shape=[
             values_shape,
@@ -252,15 +283,15 @@
             pltpu.VMEM((cols, nodes), jnp.bfloat16),
             pltpu.VMEM((device_count, width), jnp.int32),
             pltpu.VMEM((device_count, width), jnp.float32),
-            pltpu.VMEM((6, rows, cols), jnp.float32),
+            pltpu.VMEM((5, rows, cols), jnp.float32),
+            field_shape,
         ],
         in_specs=[in_vmem] * 3,
-        out_specs=[in_vmem] * 6,
+        out_specs=[in_vmem] * 7,
         scratch_shapes=[spread],
         compiler_params=params,
         name="first_values",
-    )(*vmem(exchange(message)), flat(aperture), flat(adj_source))
-    adjoint = parts[5]
+    )(*vmem(exchange(message), aperture_here, source_here))
     for _ in range(SWEEPS - 1):
         values, adjoint = pl.pallas_call(
             sweep_kernel,
@@ -270,7 +301,7 @@
             scratch_shapes=[spread],
             compiler_params=params,
             name="sweep",
-        )(*vmem(exchange(values), row_hot, col_hot, col, weight, parts, adjoint), flat(adj_source))
+        )(*vmem(exchange(values), row_hot, col_hot, col, weight, parts, adjoint, source_here))
     gradient, adjoint = pl.pallas_call(
         functools.partial(last_kernel, grid_size),
         out_shape=[jax.ShapeDtypeStruct((rows, cols), jnp.float32)] * 2,
@@ -280,8 +311,10 @@
         compiler_params=params,
         name="last_sweep",
     )(
-        *vmem(exchange(values), row_hot, col_hot, weight, parts, adjoint),
-        flat(adj_source), flat(aperture), flat(pressure),
+        *vmem(
+            exchange(values), row_hot, col_hot, weight, parts, adjoint,
+            source_here, aperture_here, pressure_here,
+        )
     )
     return gradient.reshape(aperture.shape), adjoint.reshape(aperture.shape)
 

time: 63.4 us -> 54.6 us (0.86)
  blocking collectives: 32.2 us -> 41 us
  local copies, waits for them, and re-layouts: 8.43 us -> 0 us
  waiting for transfers between devices: 6.16 us -> 0 us
  starting transfers between devices: 2.54 us -> 0 us
    all_to_all x3 -> x4, blocking collectives: 32.2 us -> 41 us  [exchange(): return lax.all_to_all(values, AXES, split_axis=0, concat_axis=0, tiled=True)]
    unnamed x24 -> x0, local copies, waits for them, and re-layouts: 7.52 us -> none
    all_to_all x1 -> x0, waiting for transfers between devices: 6.16 us -> none  [exchange(): return lax.all_to_all(values, AXES, split_axis=0, concat_axis=0, tiled=True)]
    all_to_all x1 -> x0, starting transfers between devices: 2.54 us -> none  [exchange(): return lax.all_to_all(values, AXES, split_axis=0, concat_axis=0, tiled=True)]
    squeeze x1 -> x0, local copies, waits for them, and re-layouts: 0.91 us -> none  [body(): adjoint = parts[5]]
  transfers between devices with their start and end apart: 1 -> 0, of which waited for: 1 -> 0; matrix products, arithmetic and copies ran while one was open for 1% -> 0% of each run, Pallas kernels for 0% -> 0%
where the time goes in v2:
time: 54.6 us; the launch traced here: 54.4 us
  blocking collectives  41 us (75%)
  Pallas kernels  12.7 us (23%)
  between operations  0.66 us (1%)
    all_to_all x4, blocking collectives, exchange(): return lax.all_to_all(values, AXES, split_axis=0, concat_axis=0, tiled=True)  41 us
    pallas_call x2, Pallas kernels, body(): pl.pallas_call(sweep_kernel, out_shape=[values_shape, field_shape], in_sp...  6.09 us
    pallas_call x1, Pallas kernels, body(): pl.pallas_call(functools.partial(first_kernel, grid_size), out_shape=[val...  3.34 us
    pallas_call x1, Pallas kernels, body(): pl.pallas_call(functools.partial(last_kernel, grid_size), out_shape=[jax....  2.1 us
    pallas_call x1, Pallas kernels, body(): pl.pallas_call(functools.partial(pack_kernel, grid_size * grid_size), out...  1.13 us

profile of v2, /device:TPU:0, one launch (start us, length us, event | category | flops | bytes accessed | tf_op | source)
XLA Modules:
  0.0 54.4 jit_solution(17887443050219174049)
XLA Ops:
  0.6 1.1 %pack_ends.1 = (f32[32,4,128]{2,1,0:T(4,128)S(1)}, f32[256,128]{1,0:T(8,128)S(1)}, f32[256,128]{1,0:T(8,128)S(1)}, f32[256,128]{1,0:T(8,128)S(1)}) custom-call(s32[2,16]{1,0:T(2,128)} %bitcast.10, s32[2,16]{1,0:T(2,128)} %bitcast.11, s32[16,2,64]{2,1,0:T(2,128)} %nodes_hbm.1, f32[16,64]{1,0:T(8,128)} %weight_hbm.1, f32[256,128]{1,0:T(8,128)} %bitcast.7, ...), custom_call_target="tpu_custom_call" | custom-call | tf_op jit(solution)/shard_map/pack_ends/pallas_call | solution.py:260
  1.8 14.5 %all_to_all.20.message_ref = f32[32,4,128]{2,1,0:T(4,128)S(1)} all-to-all(f32[32,4,128]{2,1,0:T(4,128)S(1)} %get-tuple-element.19), channel_id=1, replica_groups=mesh['wide'=8,'narrow'=4] {'wide','narrow'}, dimensions={0} | all-to-all | bytes 131072 | tf_op jit(solution)/shard_map/all_to_all | solution.py:253
  16.3 3.3 %first_values.1 = (f32[32,1,128]{2,1,0:T(1,128)S(1)}, bf16[256,4096]{1,0:T(8,128)(2,1)S(1)}, bf16[128,4096]{1,0:T(8,128)(2,1)S(1)}, s32[32,128]{1,0:T(8,128)S(1)...) custom-call(f32[32,4,128]{2,1,0:T(4,128)S(1)} %all_to_all.20.message_ref, ...), custom_call_target="tpu_custom_call" | custom-call | tf_op jit(solution)/shard_map/first_values/pallas_call | solution.py:278
  19.6 8.8 %all_to_all.21.arrived_ref = f32[32,1,128]{2,1,0:T(1,128)S(1)} all-to-all(f32[32,1,128]{2,1,0:T(1,128)S(1)} %get-tuple-element.22), channel_id=1, replica_groups=mesh['wide'=8,'narrow'=4] {'wide','narrow'}, dimensions={0} | all-to-all | bytes 32768 | tf_op jit(solution)/shard_map/all_to_all | solution.py:253
  28.5 3.0 %sweep.2 = (f32[32,1,128]{2,1,0:T(1,128)S(1)}, f32[256,128]{1,0:T(8,128)S(1)}) custom-call(f32[32,1,128]{2,1,0:T(1,128)S(1)} %all_to_all.21.arrived_ref, bf16[256,4096]{1,0:T(8,128)(2,1)S(1)} %get-tuple-element.23.row_hot_ref, bf16[128,4096]{1,0:T(8,128)(2,1)S(1)} %get-tuple-element.24.col_hot_ref, s32[32,128]{1,0:T(8,128)S(1)} %get-tuple-element.25.col_ref, ...), custom_call_target="tpu_custom_call" | custom-call | tf_op jit(solution)/shard_map/sweep/pallas_call | solution.py:296
  31.5 8.8 %all_to_all.22.arrived_ref = f32[32,1,128]{2,1,0:T(1,128)S(1)} all-to-all(f32[32,1,128]{2,1,0:T(1,128)S(1)} %get-tuple-element.29), channel_id=1, replica_groups=mesh['wide'=8,'narrow'=4] {'wide','narrow'}, dimensions={0} | all-to-all | bytes 32768 | tf_op jit(solution)/shard_map/all_to_all | solution.py:253
  40.4 3.0 %sweep.3 = (f32[32,1,128]{2,1,0:T(1,128)S(1)}, f32[256,128]{1,0:T(8,128)S(1)}) custom-call(f32[32,1,128]{2,1,0:T(1,128)S(1)} %all_to_all.22.arrived_ref, bf16[256,4096]{1,0:T(8,128)(2,1)S(1)} %get-tuple-element.23.row_hot_ref, bf16[128,4096]{1,0:T(8,128)(2,1)S(1)} %get-tuple-element.24.col_hot_ref, s32[32,128]{1,0:T(8,128)S(1)} %get-tuple-element.25.col_ref, ...), custom_call_target="tpu_custom_call" | custom-call | tf_op jit(solution)/shard_map/sweep/pallas_call | solution.py:296
  43.4 8.8 %all_to_all.23.arrived_ref = f32[32,1,128]{2,1,0:T(1,128)S(1)} all-to-all(f32[32,1,128]{2,1,0:T(1,128)S(1)} %get-tuple-element.31), channel_id=1, replica_groups=mesh['wide'=8,'narrow'=4] {'wide','narrow'}, dimensions={0} | all-to-all | bytes 32768 | tf_op jit(solution)/shard_map/all_to_all | solution.py:253
  52.3 2.1 %last_sweep.1 = (f32[256,128]{1,0:T(8,128)}, f32[256,128]{1,0:T(8,128)}) custom-call(f32[32,1,128]{2,1,0:T(1,128)S(1)} %all_to_all.23.arrived_ref, bf16[256,4096]{1,0:T(8,128)(2,1)S(1)} %get-tuple-element.23.row_hot_ref, bf16[128,4096]{1,0:T(8,128)(2,1)S(1)} %get-tuple-element.24.col_hot_ref, f32[32,128]{1,0:T(8,128)S(1)} %get-tuple-element.26.weight_ref, ...), custom_call_target="tpu_custom_call" | custom-call | tf_op jit(solution)/shard_map/last_sweep/pallas_call | solution.py:305

commit v3 on v2

v3 whole, which is shorter than its diff:
```python
import functools
import math

import jax
import jax.numpy as jnp
from jax import lax
from jax.experimental import pallas as pl
from jax.experimental.pallas import tpu as pltpu
from jax.sharding import PartitionSpec as P

SWEEPS = 3
INNER = 8
LEAKAGE = 0.25
AXES = ("wide", "narrow")
HIGH = lax.Precision.HIGHEST


def pack_kernel(
    cells_per, dest_hbm, local_hbm, nodes_hbm, weight_hbm, aperture_hbm, source_hbm, pressure_hbm,
    out_ref, aperture_ref, source_ref, pressure_ref,
    dest_ref, local_ref, nodes_ref, weight_ref, seen_ref, small_sems, large_sems,
):
    owned = nodes_ref.shape[0]
    devices, _, width = out_ref.shape
    small = [
        pltpu.make_async_copy(source, target, small_sems.at[index])
        for index, (source, target) in enumerate(
            ((dest_hbm, dest_ref), (local_hbm, local_ref), (nodes_hbm, nodes_ref), (weight_hbm, weight_ref))
        )
    ]
    large = [
        pltpu.make_async_copy(source, target, large_sems.at[index])
        for index, (source, target) in enumerate(
            ((aperture_hbm, aperture_ref), (source_hbm, source_ref), (pressure_hbm, pressure_ref))
        )
    ]
    for copy in small + large:
        copy.start()

    def clear(device, carry):
        seen_ref[device] = 0
        return carry

    lax.fori_loop(0, devices, clear, 0, unroll=8)
    out_ref[:, 0:2, :] = jnp.zeros((devices, 2, width), jnp.float32)
    out_ref[:, 2:4, :] = jnp.full((devices, 2, width), -1.0, jnp.float32)
    for copy in small:
        copy.wait()

    def place(index, carry):
        ends = [dest_ref[0, index], dest_ref[1, index]]
        weights = weight_ref[pl.ds(index, 1), :]
        for side in range(2):
            target = ends[side]
            rank = seen_ref[target]
            seen_ref[target] = rank + 1
            first = local_ref[side, index] * cells_per + 1
            cells = (nodes_ref[index, side : side + 1, :] + first).astype(jnp.float32)
            out_ref[target, pl.ds(rank, 1), :] = jnp.concatenate([cells, weights], axis=1)
            out_ref[target, pl.ds(rank + 2, 1), :] = jnp.full(
                (1, width), ends[1 - side].astype(jnp.float32)
            )
        return carry

    lax.fori_loop(0, owned, place, 0, unroll=True)
    for copy in large:
        copy.wait()


def face_parts(conduct, grid_size):
    rows, cols = conduct.shape
    row = lax.broadcasted_iota(jnp.int32, (rows, cols), 0) & (grid_size - 1)
    col = lax.broadcasted_iota(jnp.int32, (rows, cols), 1)
    below = jnp.where(row < grid_size - 1, (conduct + pltpu.roll(conduct, rows - 1, 0)) * 0.5, 0.0)
    above = jnp.where(row > 0, (conduct + pltpu.roll(conduct, 1, 0)) * 0.5, 0.0)
    right = jnp.where(col < cols - 1, (conduct + pltpu.roll(conduct, cols - 1, 1)) * 0.5, 0.0)
    left = jnp.where(col > 0, (conduct + pltpu.roll(conduct, 1, 1)) * 0.5, 0.0)
    return below, above, right, left


def shifted(field):
    rows, cols = field.shape
    return (
        pltpu.roll(field, rows - 1, 0),
        pltpu.roll(field, 1, 0),
        pltpu.roll(field, cols - 1, 1),
        pltpu.roll(field, 1, 1),
    )


def split_pair(values):
    high_part = values.astype(jnp.bfloat16)
    low_part = (values - high_part.astype(jnp.float32)).astype(jnp.bfloat16)
    return jnp.concatenate([high_part, low_part], axis=1)


def over_blocks(count_ref, blocks, work):
    per_block = count_ref.shape[0] // blocks
    work(0)
    if blocks > 1:
        needed = lax.div(count_ref[0, 0] + (per_block - 1), per_block)

        def step(block, carry):
            work(block)
            return carry

        lax.fori_loop(1, needed, step, 0)


def spread_dot(row_hot_ref, col_hot_ref, total_ref, value_ref, block):
    _, cols, lanes = col_hot_ref.shape
    width = value_ref.shape[2] // 2
    group = 2
    total = None
    for start in range(0, lanes // width, group):
        parts = [[], []]
        for device in range(start, start + group):
            hot = col_hot_ref[block, :, device * width : (device + 1) * width]
            value = value_ref[block, device : device + 1, :]
            for index in range(2):
                parts[index].append(hot * value[:, index * width : (index + 1) * width])
        right = jnp.concatenate([jnp.concatenate(part, axis=1) for part in parts], axis=0)
        product = lax.dot_general(
            row_hot_ref[block, :, start * width : (start + group) * width],
            right,
            (((1,), (1,)), ((), ())),
            preferred_element_type=jnp.float32,
        )
        total = product if total is None else total + product
    total = total[:, :cols] + total[:, cols:]
    if isinstance(block, int):
        total_ref[...] = total
    else:
        total_ref[...] += total


def gather(row_hot_ref, col_ref, both_ref, picked_ref, block):
    lanes = row_hot_ref.shape[2]
    _, per_block, width = picked_ref.shape
    cols = both_ref.shape[0] // 2
    group = 2
    col_ids = lax.broadcasted_iota(jnp.int32, (cols, width), 0)
    both = both_ref[...]
    for start in range(0, per_block, group):
        picked = jnp.dot(
            both,
            row_hot_ref[block, :, start * width : (start + group) * width],
            preferred_element_type=jnp.float32,
        )
        picked = picked[:cols] + picked[cols:]
        for offset in range(group):
            device = start + offset
            mine = picked[:, offset * width : (offset + 1) * width]
            hit = col_ids == col_ref[block, device : device + 1, :]
            picked_ref[block, device : device + 1, :] = jnp.sum(
                jnp.where(hit, mine, 0.0), axis=0, keepdims=True
            )


def send_values(adjoint, row_hot_ref, col_ref, count_ref, order_ref, both_ref, picked_ref, values_ref):
    blocks, per_block, width = picked_ref.shape
    devices = blocks * per_block
    turned = split_pair(adjoint.T)
    rows = adjoint.shape[0]
    both_ref[...] = jnp.concatenate([turned[:, :rows], turned[:, rows:]], axis=0)
    if blocks > 1:
        picked_ref[1:] = jnp.zeros((blocks - 1, per_block, width), jnp.float32)
    over_blocks(count_ref, blocks, lambda block: gather(row_hot_ref, col_ref, both_ref, picked_ref, block))
    picked = split_pair(picked_ref[...].reshape(devices, width))
    sent = jnp.dot(order_ref[1, :, :devices], picked, preferred_element_type=jnp.float32)
    values_ref[:, 0, :] = sent[:, :width] + sent[:, width:]


def first_kernel(
    grid_size, message_ref, aperture_ref, source_ref,
    values_ref, row_hot_ref, col_hot_ref, col_ref, weight_ref, count_ref, order_ref, parts_ref, adjoint_ref,
    row_ref, value_ref, total_ref, both_ref, picked_ref,
):
    devices, _, width = message_ref.shape
    trace_len = width // 2
    blocks, per_block, _ = col_ref.shape
    rows, cols = aperture_ref.shape
    slots = [message_ref[:, rank, :] for rank in range(2)]
    partners = [message_ref[:, 2 + rank, :] for rank in range(2)]
    down = lax.broadcasted_iota(jnp.int32, (devices, width), 0)
    along = lax.broadcasted_iota(jnp.int32, (devices, width), 1)
    partner_along = [
        jnp.sum(jnp.where(down == along, partners[rank], 0.0), axis=0, keepdims=True) for rank in range(2)
    ]
    device_id = down.astype(jnp.float32)
    ordered = [jnp.zeros((devices, width), jnp.float32) for _ in range(2)]
    for rank in range(2):
        same = [partners[other] == partner_along[rank] for other in range(2)]
        ahead = (down < along) if rank == 0 else (down <= along)
        earlier = jnp.where(same[0] & ahead, 1.0, 0.0) + jnp.where(same[1] & (down < along), 1.0, 0.0)
        position = jnp.sum(earlier, axis=0, keepdims=True)
        for spot in range(2):
            pick = jnp.where((device_id == partner_along[rank]) & (position == float(spot)), 1.0, 0.0)
            ordered[spot] = ordered[spot] + jnp.dot(
                pick[:, :devices], slots[rank], precision=HIGH, preferred_element_type=jnp.float32
            )
    front = along < trace_len
    cell = jnp.where(front, ordered[0], pltpu.roll(ordered[1], trace_len, 1)).astype(jnp.int32) - 1
    weight = jnp.where(front, pltpu.roll(ordered[0], trace_len, 1), ordered[1])
    weight_ref[...] = weight
    used_down = jnp.max(jnp.where(cell >= 0, 1.0, 0.0), axis=1, keepdims=True)
    used_along = jnp.sum(jnp.where(down == along, used_down, 0.0), axis=0, keepdims=True)
    place_along = jnp.sum(jnp.where(down < along, used_down, 0.0), axis=0, keepdims=True)
    place_down = jnp.sum(jnp.where(along < down, used_along, 0.0), axis=1, keepdims=True)
    count_ref[...] = jnp.broadcast_to(jnp.sum(used_down, axis=0, keepdims=True), count_ref.shape).astype(jnp.int32)
    order_ref[0] = jnp.where((device_id == place_along) & (used_along > 0.5), 1.0, 0.0).astype(jnp.bfloat16)
    order_ref[1] = jnp.where((along.astype(jnp.float32) == place_down) & (used_down > 0.5), 1.0, 0.0).astype(
        jnp.bfloat16
    )
    row = (cell >> (grid_size.bit_length() - 1)).astype(jnp.float32).astype(jnp.bfloat16)
    col = (cell & (grid_size - 1)).astype(jnp.float32).astype(jnp.bfloat16)
    packed = jnp.dot(
        order_ref[0, :, :devices],
        jnp.concatenate([row, col, split_pair(weight)], axis=1),
        preferred_element_type=jnp.float32,
    )
    row_ref[...] = packed[:, :width].astype(jnp.bfloat16).reshape(row_ref.shape)
    col_ref[...] = packed[:, width : 2 * width].astype(jnp.int32).reshape(col_ref.shape)
    value_ref[...] = packed[:, 2 * width :].astype(jnp.bfloat16).reshape(value_ref.shape)
    cell_ids = lax.broadcasted_iota(jnp.int32, (rows, width), 0).astype(jnp.float32).astype(jnp.bfloat16)
    one, zero = jnp.ones((), jnp.bfloat16), jnp.zeros((), jnp.bfloat16)

    def build(block):
        block_cols = col_ref[block].astype(jnp.float32).astype(jnp.bfloat16)
        block_rows = row_ref[block]
        for device in range(per_block):
            lanes = slice(device * width, (device + 1) * width)
            row_hot_ref[block, :, lanes] = jnp.where(cell_ids == block_rows[device : device + 1], one, zero)
            col_hot_ref[block, :, lanes] = jnp.where(
                cell_ids[:cols] == block_cols[device : device + 1], one, zero
            )
        spread_dot(row_hot_ref, col_hot_ref, total_ref, value_ref, block)

    over_blocks(count_ref, blocks, build)
    aperture = aperture_ref[...]
    faces = face_parts(aperture * aperture * aperture / 12.0, grid_size)
    inv_diag = 1.0 / (LEAKAGE + (faces[0] + faces[1] + faces[2] + faces[3]) + total_ref[...])
    for index in range(4):
        parts_ref[index] = faces[index] * inv_diag
    parts_ref[4] = inv_diag
    adjoint = source_ref[...] * inv_diag
    adjoint_ref[...] = adjoint
    send_values(adjoint, row_hot_ref, col_ref, count_ref, order_ref, both_ref, picked_ref, values_ref)


def relax(
    arrived_ref, row_hot_ref, col_hot_ref, weight_ref, count_ref, order_ref, parts_ref, start_ref, source_ref,
    value_ref, total_ref,
):
    blocks = value_ref.shape[0]
    devices = arrived_ref.shape[0]
    terms = split_pair(weight_ref[...] * arrived_ref[:, 0, :])
    placed = jnp.dot(order_ref[0, :, :devices], terms, preferred_element_type=jnp.float32)
    value_ref[...] = placed.astype(jnp.bfloat16).reshape(value_ref.shape)
    over_blocks(
        count_ref, blocks, lambda block: spread_dot(row_hot_ref, col_hot_ref, total_ref, value_ref, block)
    )
    forcing = (source_ref[...] + total_ref[...]) * parts_ref[4]
    adjoint = start_ref[...]
    for _ in range(INNER):
        below, above, right, left = shifted(adjoint)
        adjoint = (
            forcing + (parts_ref[0] * below + parts_ref[1] * above)
            + (parts_ref[2] * right + parts_ref[3] * left)
        )
    return adjoint


def sweep_kernel(
    arrived_ref, row_hot_ref, col_hot_ref, col_ref, weight_ref, count_ref, order_ref, parts_ref, start_ref,
    source_ref, values_ref, adjoint_ref, value_ref, total_ref, both_ref, picked_ref,
):
    adjoint = relax(
        arrived_ref, row_hot_ref, col_hot_ref, weight_ref, count_ref, order_ref, parts_ref, start_ref, source_ref,
        value_ref, total_ref,
    )
    adjoint_ref[...] = adjoint
    send_values(adjoint, row_hot_ref, col_ref, count_ref, order_ref, both_ref, picked_ref, values_ref)


def last_kernel(
    grid_size, arrived_ref, row_hot_ref, col_hot_ref, weight_ref, count_ref, order_ref, parts_ref, start_ref,
    source_ref, aperture_ref, pressure_ref, gradient_ref, adjoint_ref, value_ref, total_ref,
):
    adjoint = relax(
        arrived_ref, row_hot_ref, col_hot_ref, weight_ref, count_ref, order_ref, parts_ref, start_ref, source_ref,
        value_ref, total_ref,
    )
    adjoint_ref[...] = adjoint
    pressure = pressure_ref[...]
    rows, cols = adjoint.shape
    row = lax.broadcasted_iota(jnp.int32, (rows, cols), 0) & (grid_size - 1)
    col = lax.broadcasted_iota(jnp.int32, (rows, cols), 1)
    inside = (row < grid_size - 1, row > 0, col < cols - 1, col > 0)
    total = jnp.zeros((rows, cols), jnp.float32)
    for keep, near_pressure, near_adjoint in zip(inside, shifted(pressure), shifted(adjoint), strict=True):
        total = total + jnp.where(keep, (pressure - near_pressure) * (adjoint - near_adjoint), 0.0)
    aperture = aperture_ref[...]
    gradient_ref[...] = -(aperture * aperture / 8.0) * total


def body(aperture, pressure, adj_source, trace_weight, end_device, end_local, trace_nodes):
    frac_count, grid_size, _ = aperture.shape
    owned_count, trace_len = trace_weight.shape
    device_count = lax.axis_size(AXES)
    rows, cols, width = frac_count * grid_size, grid_size, 2 * trace_len
    nodes = device_count * width
    per_block = math.gcd(device_count, 16)
    blocks = device_count // per_block
    in_vmem = pl.BlockSpec(memory_space=pltpu.VMEM)
    in_hbm = pl.BlockSpec(memory_space=pltpu.HBM)
    params = pltpu.CompilerParams(vmem_limit_bytes=(8 << 20) + nodes * 1024)
    landing = [
        pltpu.VMEM((blocks, per_block, 2 * width), jnp.bfloat16),
        pltpu.VMEM((rows, cols), jnp.float32),
    ]
    leaving = [
        pltpu.VMEM((2 * cols, rows), jnp.bfloat16),
        pltpu.VMEM((blocks, per_block, width), jnp.float32),
    ]

    def flat(field):
        return field.reshape(rows, cols)

    def vmem(*arrays):
        return [pltpu.with_memory_space_constraint(array, pltpu.VMEM) for array in arrays]

    def exchange(values):
        return lax.all_to_all(values, AXES, split_axis=0, concat_axis=0, tiled=True)

    field_shape = pltpu.VMEM((rows, cols), jnp.float32)
    arguments = (
        end_device.T, end_local.T, trace_nodes, trace_weight, flat(aperture), flat(adj_source), flat(pressure)
    )
    message, aperture_here, source_here, pressure_here = pl.pallas_call(
        functools.partial(pack_kernel, grid_size * grid_size),
        out_shape=[pltpu.VMEM((device_count, 4, width), jnp.float32)] + [field_shape] * 3,
        in_specs=[in_hbm] * 7,
        out_specs=[in_vmem] * 4,
        scratch_shapes=[
            pltpu.SMEM((2, owned_count), jnp.int32),
            pltpu.SMEM((2, owned_count), jnp.int32),
            pltpu.VMEM(trace_nodes.shape, jnp.int32),
            pltpu.VMEM(trace_weight.shape, jnp.float32),
            pltpu.SMEM((device_count,), jnp.int32),
            pltpu.SemaphoreType.DMA((4,)),
            pltpu.SemaphoreType.DMA((3,)),
        ],
        compiler_params=params,
        name="pack_ends",
    )(*[pltpu.with_memory_space_constraint(array, pltpu.HBM) for array in arguments])
    values_shape = pltpu.VMEM((device_count, 1, width), jnp.float32)
    values, row_hot, col_hot, col, weight, count, order, parts, adjoint = pl.pallas_call(
        functools.partial(first_kernel, grid_size),
        out_shape=[
            values_shape,
            pltpu.VMEM((blocks, rows, per_block * width), jnp.bfloat16),
            pltpu.VMEM((blocks, cols, per_block * width), jnp.bfloat16),
            pltpu.VMEM((blocks, per_block, width), jnp.int32),
            pltpu.VMEM((device_count, width), jnp.float32),
            pltpu.VMEM((device_count, width), jnp.int32),
            pltpu.VMEM((2, device_count, width), jnp.bfloat16),
            pltpu.VMEM((5, rows, cols), jnp.float32),
            field_shape,
        ],
        in_specs=[in_vmem] * 3,
        out_specs=[in_vmem] * 9,
        scratch_shapes=[pltpu.VMEM((blocks, per_block, width), jnp.bfloat16)] + landing + leaving,
        compiler_params=params,
        name="first_values",
    )(*vmem(exchange(message), aperture_here, source_here))
    for _ in range(SWEEPS - 1):
        values, adjoint = pl.pallas_call(
            sweep_kernel,
            out_shape=[values_shape, field_shape],
            in_specs=[in_vmem] * 10,
            out_specs=[in_vmem] * 2,
            scratch_shapes=landing + leaving,
            compiler_params=params,
            name="sweep",
        )(
            *vmem(
                exchange(values), row_hot, col_hot, col, weight, count, order, parts, adjoint, source_here
            )
        )
    gradient, adjoint = pl.pallas_call(
        functools.partial(last_kernel, grid_size),
        out_shape=[jax.ShapeDtypeStruct((rows, cols), jnp.float32)] * 2,
        in_specs=[in_vmem] * 11,
        out_specs=[in_vmem] * 2,
        scratch_shapes=landing,
        compiler_params=params,
        name="last_sweep",
    )(
        *vmem(
            exchange(values), row_hot, col_hot, weight, count, order, parts, adjoint,
            source_here, aperture_here, pressure_here,
        )
    )
    return gradient.reshape(aperture.shape), adjoint.reshape(aperture.shape)


def solution(mesh):
    fields, pairs = P(AXES, None, None), P(AXES, None)
    return jax.shard_map(
        body,
        mesh=mesh,
        in_specs=(fields, fields, fields, pairs, pairs, pairs, fields),
        out_specs=(fields, fields),
        check_vma=False,
    )
```

time: 54.6 us -> 51.2 us (0.938)
  Pallas kernels: 12.7 us -> 9.28 us
    pallas_call x2, Pallas kernels: 6.09 us -> 3.77 us  [body(): pl.pallas_call(sweep_kernel, out_shape=[values_shape, field_shape], in_sp...]
    pallas_call x1, Pallas kernels: 3.34 us -> 2.02 us  [body(): pl.pallas_call(functools.partial(first_kernel, grid_size), out_shape=[val...]
where the time goes in v3:
time: 51.2 us; the launch traced here: 51 us
  blocking collectives  41 us (80%)
  Pallas kernels  9.28 us (18%)
  between operations  0.66 us (1%)
    all_to_all x4, blocking collectives, exchange(): return lax.all_to_all(values, AXES, split_axis=0, concat_axis=0, tiled=True)  41 us
    pallas_call x2, Pallas kernels, body(): pl.pallas_call(sweep_kernel, out_shape=[values_shape, field_shape], in_sp...  3.77 us
    pallas_call x1, Pallas kernels, body(): pl.pallas_call(functools.partial(last_kernel, grid_size), out_shape=[jax....  2.36 us
    pallas_call x1, Pallas kernels, body(): pl.pallas_call(functools.partial(first_kernel, grid_size), out_shape=[val...  2.02 us
    pallas_call x1, Pallas kernels, body(): pl.pallas_call(functools.partial(pack_kernel, grid_size * grid_size), out...  1.13 us

profile of v3, /device:TPU:0, one launch (start us, length us, event | category | flops | bytes accessed | tf_op | source)
XLA Modules:
  0.0 51.0 jit_solution(10957633002072816098)
XLA Ops:
  0.6 1.1 %pack_ends.1 = (f32[32,4,128]{2,1,0:T(4,128)S(1)}, f32[256,128]{1,0:T(8,128)S(1)}, f32[256,128]{1,0:T(8,128)S(1)}, f32[256,128]{1,0:T(8,128)S(1)}) custom-call(s32[2,16]{1,0:T(2,128)} %bitcast.10, s32[2,16]{1,0:T(2,128)} %bitcast.11, s32[16,2,64]{2,1,0:T(2,128)} %nodes_hbm.1, f32[16,64]{1,0:T(8,128)} %weight_hbm.1, f32[256,128]{1,0:T(8,128)} %bitcast.7, ...), custom_call_target="tpu_custom_call" | custom-call | tf_op jit(solution)/shard_map/pack_ends/pallas_call | solution.py:340
  1.8 14.5 %all_to_all.20.message_ref = f32[32,4,128]{2,1,0:T(4,128)S(1)} all-to-all(f32[32,4,128]{2,1,0:T(4,128)S(1)} %get-tuple-element.21), channel_id=1, replica_groups=mesh['wide'=8,'narrow'=4] {'wide','narrow'}, dimensions={0} | all-to-all | bytes 131072 | tf_op jit(solution)/shard_map/all_to_all | solution.py:334
  16.3 2.0 %first_values.1 = (f32[32,1,128]{2,1,0:T(1,128)S(1)}, bf16[2,256,2048]{2,1,0:T(8,128)(2,1)S(1)}, bf16[2,128,2048]{2,1,0:T(8,128)(2,1)S(1)}, s32[2,16,128]{2,1,0:...) custom-call(f32[32,4,128]{2,1,0:T(4,128)S(1)} %all_to_all.20.message, ...), custom_call_target="tpu_custom_call" | custom-call | tf_op jit(solution)/shard_map/first_values/pallas_call | solution.py:358
  18.3 8.8 %all_to_all.21.arrived_ref = f32[32,1,128]{2,1,0:T(1,128)S(1)} all-to-all(f32[32,1,128]{2,1,0:T(1,128)S(1)} %get-tuple-element.24), channel_id=1, replica_groups=mesh['wide'=8,'narrow'=4] {'wide','narrow'}, dimensions={0} | all-to-all | bytes 32768 | tf_op jit(solution)/shard_map/all_to_all | solution.py:334
  27.2 1.9 %sweep.2 = (f32[32,1,128]{2,1,0:T(1,128)S(1)}, f32[256,128]{1,0:T(8,128)S(1)}) custom-call(f32[32,1,128]{2,1,0:T(1,128)S(1)} %all_to_all.21.arrived_ref, bf16[2,256,2048]{2,1,0:T(8,128)(2,1)S(1)} %get-tuple-element.25.row_hot_ref, bf16[2,128,2048]{2,1,0:T(8,128)(2,1)S(1)} %get-tuple-element.26.col_hot_ref, s32[2,16,128]{2,1,0:T(8,128)S(1)} %get-tuple-element.27.col_ref, ...), custom_call_target="tpu_custom_call" | custom-call | tf_op jit(solution)/shard_map/sweep/pallas_call | solution.py:378
  29.1 8.8 %all_to_all.22.arrived_ref = f32[32,1,128]{2,1,0:T(1,128)S(1)} all-to-all(f32[32,1,128]{2,1,0:T(1,128)S(1)} %get-tuple-element.33), channel_id=1, replica_groups=mesh['wide'=8,'narrow'=4] {'wide','narrow'}, dimensions={0} | all-to-all | bytes 32768 | tf_op jit(solution)/shard_map/all_to_all | solution.py:334
  37.9 1.9 %sweep.3 = (f32[32,1,128]{2,1,0:T(1,128)S(1)}, f32[256,128]{1,0:T(8,128)S(1)}) custom-call(f32[32,1,128]{2,1,0:T(1,128)S(1)} %all_to_all.22.arrived_ref, bf16[2,256,2048]{2,1,0:T(8,128)(2,1)S(1)} %get-tuple-element.25.row_hot_ref, bf16[2,128,2048]{2,1,0:T(8,128)(2,1)S(1)} %get-tuple-element.26.col_hot_ref, s32[2,16,128]{2,1,0:T(8,128)S(1)} %get-tuple-element.27.col_ref, ...), custom_call_target="tpu_custom_call" | custom-call | tf_op jit(solution)/shard_map/sweep/pallas_call | solution.py:378
  39.8 8.8 %all_to_all.23.arrived_ref = f32[32,1,128]{2,1,0:T(1,128)S(1)} all-to-all(f32[32,1,128]{2,1,0:T(1,128)S(1)} %get-tuple-element.35), channel_id=1, replica_groups=mesh['wide'=8,'narrow'=4] {'wide','narrow'}, dimensions={0} | all-to-all | bytes 32768 | tf_op jit(solution)/shard_map/all_to_all | solution.py:334
  48.6 2.4 %last_sweep.1 = (f32[256,128]{1,0:T(8,128)}, f32[256,128]{1,0:T(8,128)}) custom-call(f32[32,1,128]{2,1,0:T(1,128)S(1)} %all_to_all.23.arrived_ref, bf16[2,256,2048]{2,1,0:T(8,128)(2,1)S(1)} %get-tuple-element.25.row_hot_ref, bf16[2,128,2048]{2,1,0:T(8,128)(2,1)S(1)} %get-tuple-element.26.col_hot_ref, f32[32,128]{1,0:T(8,128)S(1)} %get-tuple-element.28.weight_ref, ...), custom_call_target="tpu_custom_call" | custom-call | tf_op jit(solution)/shard_map/last_sweep/pallas_call | solution.py:391

commit v4 on v3

v4 whole, which is shorter than its diff:
```python
import functools
import math

import jax
import jax.numpy as jnp
from jax import lax
from jax.experimental import pallas as pl
from jax.experimental.pallas import tpu as pltpu
from jax.sharding import PartitionSpec as P

SWEEPS = 3
INNER = 8
LEAKAGE = 0.25
AXES = ("wide", "narrow")
SLICE = 8


def pack_kernel(
    cells_per, dest_hbm, local_hbm, nodes_hbm, weight_hbm, aperture_hbm, source_hbm, pressure_hbm,
    out_ref, aperture_ref, source_ref, pressure_ref,
    dest_ref, local_ref, nodes_ref, weight_ref, seen_ref, small_sems, large_sems,
):
    owned = nodes_ref.shape[0]
    devices, _, width = out_ref.shape
    small = [
        pltpu.make_async_copy(source, target, small_sems.at[index])
        for index, (source, target) in enumerate(
            ((dest_hbm, dest_ref), (local_hbm, local_ref), (nodes_hbm, nodes_ref), (weight_hbm, weight_ref))
        )
    ]
    large = [
        pltpu.make_async_copy(source, target, large_sems.at[index])
        for index, (source, target) in enumerate(
            ((aperture_hbm, aperture_ref), (source_hbm, source_ref), (pressure_hbm, pressure_ref))
        )
    ]
    for copy in small + large:
        copy.start()

    def clear(device, carry):
        seen_ref[device] = 0
        return carry

    lax.fori_loop(0, devices, clear, 0, unroll=8)
    out_ref[:, 0:2, :] = jnp.zeros((devices, 2, width), jnp.float32)
    out_ref[:, 2:4, :] = jnp.full((devices, 2, width), -1.0, jnp.float32)
    for copy in small:
        copy.wait()

    def place(index, carry):
        ends = [dest_ref[0, index], dest_ref[1, index]]
        weights = weight_ref[pl.ds(index, 1), :]
        for side in range(2):
            target = ends[side]
            rank = seen_ref[target]
            seen_ref[target] = rank + 1
            first = local_ref[side, index] * cells_per + 1
            cells = (nodes_ref[index, side : side + 1, :] + first).astype(jnp.float32)
            out_ref[target, pl.ds(rank, 1), :] = jnp.concatenate([cells, weights], axis=1)
            out_ref[target, pl.ds(rank + 2, 1), :] = jnp.full(
                (1, width), ends[1 - side].astype(jnp.float32)
            )
        return carry

    lax.fori_loop(0, owned, place, 0, unroll=True)
    for copy in large:
        copy.wait()


def face_parts(conduct, grid_size):
    rows, cols = conduct.shape
    row = lax.broadcasted_iota(jnp.int32, (rows, cols), 0) & (grid_size - 1)
    col = lax.broadcasted_iota(jnp.int32, (rows, cols), 1)
    below = jnp.where(row < grid_size - 1, (conduct + pltpu.roll(conduct, rows - 1, 0)) * 0.5, 0.0)
    above = jnp.where(row > 0, (conduct + pltpu.roll(conduct, 1, 0)) * 0.5, 0.0)
    right = jnp.where(col < cols - 1, (conduct + pltpu.roll(conduct, cols - 1, 1)) * 0.5, 0.0)
    left = jnp.where(col > 0, (conduct + pltpu.roll(conduct, 1, 1)) * 0.5, 0.0)
    return below, above, right, left


def split_pair(values):
    high_part = values.astype(jnp.bfloat16)
    low_part = (values - high_part.astype(jnp.float32)).astype(jnp.bfloat16)
    return high_part, low_part


def split_three(values):
    high_part, low_part = split_pair(values)
    rest = values - high_part.astype(jnp.float32) - low_part.astype(jnp.float32)
    return high_part, low_part, rest.astype(jnp.bfloat16)


def over_blocks(count_ref, blocks, work):
    per_block = count_ref.shape[0] // blocks
    work(0)
    if blocks > 1:
        needed = lax.div(count_ref[0, 0] + (per_block - 1), per_block)

        def step(block, carry):
            work(block)
            return carry

        lax.fori_loop(1, needed, step, 0)


def spread(row_hot_ref, col_hot_ref, total_ref, value_of, block):
    _, cols, lanes = col_hot_ref.shape
    group = 2
    width = value_of(block, 0).shape[1]
    total = None
    for start in range(0, lanes // width, group):
        parts = [[], []]
        for device in range(start, start + group):
            hot = col_hot_ref[block, :, device * width : (device + 1) * width]
            for part, value in zip(parts, split_pair(value_of(block, device)), strict=True):
                part.append(hot * value)
        right = jnp.concatenate([jnp.concatenate(part, axis=1) for part in parts], axis=0)
        product = lax.dot_general(
            row_hot_ref[block, :, start * width : (start + group) * width],
            right,
            (((1,), (1,)), ((), ())),
            preferred_element_type=jnp.float32,
        )
        total = product if total is None else total + product
    total = total[:, :cols] + total[:, cols:]
    if isinstance(block, int):
        total_ref[...] = total
    else:
        total_ref[...] += total


def gather(row_hot_ref, col_ref, peer_ref, both_ref, values_ref, block):
    _, per_block, width = col_ref.shape
    cols = both_ref.shape[0] // 2
    group = 2
    col_ids = lax.broadcasted_iota(jnp.int32, (cols, width), 0)
    both = both_ref[...]
    for start in range(0, per_block, group):
        picked = jnp.dot(
            both,
            row_hot_ref[block, :, start * width : (start + group) * width],
            preferred_element_type=jnp.float32,
        )
        picked = picked[:cols] + picked[cols:]
        for offset in range(group):
            device = start + offset
            mine = picked[:, offset * width : (offset + 1) * width]
            hit = col_ids == col_ref[block, device : device + 1, :]
            values_ref[peer_ref[block, device, 0]] = jnp.sum(
                jnp.where(hit, mine, 0.0), axis=0, keepdims=True
            )


def send_values(adjoint, row_hot_ref, col_ref, count_ref, peer_ref, both_ref, values_ref):
    values_ref[...] = jnp.zeros(values_ref.shape, jnp.float32)
    both_ref[...] = jnp.concatenate(split_pair(adjoint.T), axis=0)
    over_blocks(
        count_ref, col_ref.shape[0],
        lambda block: gather(row_hot_ref, col_ref, peer_ref, both_ref, values_ref, block),
    )


def first_kernel(
    grid_size, message_ref, aperture_ref, source_ref,
    values_ref, row_hot_ref, col_hot_ref, col_ref, weight_ref, count_ref, peer_ref, parts_ref, adjoint_ref,
    row_ref, total_ref, both_ref,
):
    devices, _, width = message_ref.shape
    trace_len = width // 2
    blocks, per_block, _ = col_ref.shape
    rows, cols = aperture_ref.shape
    slots = [message_ref[:, rank, :] for rank in range(2)]
    partners = [message_ref[:, 2 + rank, :] for rank in range(2)]
    down = lax.broadcasted_iota(jnp.int32, (devices, width), 0)
    along = lax.broadcasted_iota(jnp.int32, (devices, width), 1)
    device_id = down.astype(jnp.float32)
    target = [
        jnp.sum(jnp.where(down == along, partners[rank], 0.0), axis=0, keepdims=True) for rank in range(2)
    ]
    target = [jnp.where(along[0:1] < devices, target[rank], -1.0) for rank in range(2)]
    used = jnp.where((device_id == target[0]) | (device_id == target[1]), 1.0, 0.0)
    used = jnp.max(used, axis=1, keepdims=True)
    count = jnp.sum(used, axis=0, keepdims=True)
    packed = jnp.zeros((2 * devices, 4 * width), jnp.float32)
    for rank in range(2):
        place = jnp.sum(jnp.where(device_id < target[rank], used, 0.0), axis=0, keepdims=True)
        ahead = (down < along) if rank == 0 else (down <= along)
        earlier = jnp.where((partners[0] == target[rank]) & ahead, 1.0, 0.0)
        earlier = earlier + jnp.where((partners[1] == target[rank]) & (down < along), 1.0, 0.0)
        spot = jnp.sum(earlier, axis=0, keepdims=True)
        here = (device_id == place) & (target[rank] >= 0.0)
        pick = [jnp.where(here & (spot == float(index)), 1.0, 0.0).astype(jnp.bfloat16) for index in range(2)]
        packed = packed + jnp.dot(
            jnp.concatenate(pick, axis=0)[:, :devices],
            jnp.concatenate(split_three(slots[rank]) + (partners[rank].astype(jnp.bfloat16),), axis=1),
            preferred_element_type=jnp.float32,
        )
    ends = packed[:, :width] + packed[:, width : 2 * width] + packed[:, 2 * width : 3 * width]
    ends = [ends[:devices], ends[devices:]]
    front = along < trace_len
    cell = jnp.where(front, ends[0], pltpu.roll(ends[1], trace_len, 1)).astype(jnp.int32) - 1
    weight = jnp.where(front, pltpu.roll(ends[0], trace_len, 1), ends[1])
    me = lax.axis_index(AXES)
    peer = jnp.where(device_id < count, packed[:devices, 3 * width :].astype(jnp.int32), me)
    count_ref[...] = jnp.broadcast_to(count, count_ref.shape).astype(jnp.int32)
    peer_ref[...] = peer.reshape(peer_ref.shape)
    weight_ref[...] = weight.reshape(weight_ref.shape)
    row_ref[...] = (cell >> (grid_size.bit_length() - 1)).reshape(row_ref.shape)
    col_ref[...] = (cell & (grid_size - 1)).reshape(col_ref.shape)
    cell_ids = lax.broadcasted_iota(jnp.int32, (rows, width), 0).astype(jnp.float32).astype(jnp.bfloat16)
    one, zero = jnp.ones((), jnp.bfloat16), jnp.zeros((), jnp.bfloat16)

    def build(block):
        block_cols = col_ref[block].astype(jnp.float32).astype(jnp.bfloat16)
        block_rows = row_ref[block].astype(jnp.float32).astype(jnp.bfloat16)
        for device in range(per_block):
            lanes = slice(device * width, (device + 1) * width)
            row_hot_ref[block, :, lanes] = jnp.where(cell_ids == block_rows[device : device + 1], one, zero)
            col_hot_ref[block, :, lanes] = jnp.where(
                cell_ids[:cols] == block_cols[device : device + 1], one, zero
            )
        spread(
            row_hot_ref, col_hot_ref, total_ref,
            lambda block, device: weight_ref[block, device : device + 1, :], block,
        )

    over_blocks(count_ref, blocks, build)
    aperture = aperture_ref[...]
    faces = face_parts(aperture * aperture * aperture / 12.0, grid_size)
    inv_diag = 1.0 / (LEAKAGE + (faces[0] + faces[1] + faces[2] + faces[3]) + total_ref[...])
    for index in range(4):
        parts_ref[index] = faces[index] * inv_diag
    parts_ref[4] = inv_diag
    adjoint = source_ref[...] * inv_diag
    adjoint_ref[...] = adjoint
    send_values(adjoint, row_hot_ref, col_ref, count_ref, peer_ref, both_ref, values_ref)


def near(state_ref, rows):
    cols = state_ref.shape[1]
    first = SLICE + rows
    here = state_ref[first : first + SLICE]
    return here, (
        state_ref[first + 1 : first + SLICE + 1],
        state_ref[first - 1 : first + SLICE - 1],
        pltpu.roll(here, cols - 1, 1),
        pltpu.roll(here, 1, 1),
    )


def relax(
    arrived_ref, row_hot_ref, col_hot_ref, weight_ref, count_ref, peer_ref, parts_ref, start_ref, source_ref,
    adjoint_ref, total_ref, early_ref, state_ref, before_ref=None,
):
    rows, cols = start_ref.shape
    slices = range(0, rows, SLICE)
    margin = jnp.zeros((SLICE, cols), jnp.float32)
    for index in range(2):
        state_ref[index, 0:SLICE] = margin
        state_ref[index, SLICE + rows :] = margin
    state_ref[0, SLICE : SLICE + rows] = start_ref[...]

    def pull(state, first):
        _, (below, above, right, left) = near(state, first)
        here = slice(first, first + SLICE)
        return (parts_ref[0, here] * below + parts_ref[1, here] * above) + (
            parts_ref[2, here] * right + parts_ref[3, here] * left
        )

    for first in slices:
        early_ref[first : first + SLICE] = pull(state_ref.at[0], first)
    if before_ref is not None:
        before_ref()
    over_blocks(
        count_ref, weight_ref.shape[0],
        lambda block: spread(
            row_hot_ref, col_hot_ref, total_ref,
            lambda block, device: weight_ref[block, device : device + 1, :] * arrived_ref[peer_ref[block, device, 0]],
            block,
        ),
    )
    for step in range(INNER):
        old, new = state_ref.at[step % 2], state_ref.at[(step + 1) % 2]
        for first in slices:
            here = slice(first, first + SLICE)
            if step == 0:
                forcing = (source_ref[here] + total_ref[here]) * parts_ref[4, here]
                total_ref[here] = forcing
                now = forcing + early_ref[here]
            else:
                now = total_ref[here] + pull(old, first)
            new[SLICE + first : 2 * SLICE + first] = now
            if step == INNER - 1:
                adjoint_ref[here] = now


def sweep_kernel(
    arrived_ref, row_hot_ref, col_hot_ref, col_ref, weight_ref, count_ref, peer_ref, parts_ref, start_ref,
    source_ref, values_ref, adjoint_ref, total_ref, early_ref, state_ref, both_ref,
):
    relax(
        arrived_ref, row_hot_ref, col_hot_ref, weight_ref, count_ref, peer_ref, parts_ref, start_ref, source_ref,
        adjoint_ref, total_ref, early_ref, state_ref,
    )
    send_values(adjoint_ref[...], row_hot_ref, col_ref, count_ref, peer_ref, both_ref, values_ref)


def last_kernel(
    grid_size, arrived_ref, row_hot_ref, col_hot_ref, weight_ref, count_ref, peer_ref, parts_ref, start_ref,
    source_ref, aperture_ref, pressure_ref, gradient_hbm, adjoint_hbm,
    total_ref, early_ref, state_ref, share_ref, gradient_ref, adjoint_ref, sems,
):
    rows, cols = start_ref.shape
    slices = range(0, rows, SLICE)

    def shares():
        aperture = aperture_ref[...]
        scale = -(aperture * aperture / 8.0)
        pressure = pressure_ref[...]
        row = lax.broadcasted_iota(jnp.int32, (rows, cols), 0) & (grid_size - 1)
        col = lax.broadcasted_iota(jnp.int32, (rows, cols), 1)
        inside = (row < grid_size - 1, row > 0, col < cols - 1, col > 0)
        turns = ((rows - 1, 0), (1, 0), (cols - 1, 1), (1, 1))
        for index in range(4):
            share_ref[index] = jnp.where(
                inside[index], scale * (pressure - pltpu.roll(pressure, *turns[index])), 0.0
            )

    relax(
        arrived_ref, row_hot_ref, col_hot_ref, weight_ref, count_ref, peer_ref, parts_ref, start_ref, source_ref,
        adjoint_ref, total_ref, early_ref, state_ref, shares,
    )
    keep = pltpu.make_async_copy(adjoint_ref, adjoint_hbm, sems.at[0])
    keep.start()
    last_state = state_ref.at[INNER % 2]
    for first in slices:
        here, sides = near(last_state, first)
        lines = slice(first, first + SLICE)
        terms = [share_ref[index, lines] * (here - side) for index, side in enumerate(sides)]
        gradient_ref[lines] = (terms[0] + terms[1]) + (terms[2] + terms[3])
    send = pltpu.make_async_copy(gradient_ref, gradient_hbm, sems.at[1])
    send.start()
    keep.wait()
    send.wait()


def body(aperture, pressure, adj_source, trace_weight, end_device, end_local, trace_nodes):
    frac_count, grid_size, _ = aperture.shape
    owned_count, trace_len = trace_weight.shape
    device_count = lax.axis_size(AXES)
    rows, cols, width = frac_count * grid_size, grid_size, 2 * trace_len
    nodes = device_count * width
    per_block = math.gcd(device_count, 16)
    blocks = device_count // per_block
    in_vmem = pl.BlockSpec(memory_space=pltpu.VMEM)
    in_hbm = pl.BlockSpec(memory_space=pltpu.HBM)
    params = pltpu.CompilerParams(vmem_limit_bytes=(8 << 20) + nodes * 1024)
    field = pltpu.VMEM((rows, cols), jnp.float32)
    sweeping = [field, field, pltpu.VMEM((2, rows + 2 * SLICE, cols), jnp.float32)]
    leaving = [pltpu.VMEM((2 * cols, rows), jnp.bfloat16)]
    ends_int = pltpu.VMEM((blocks, per_block, width), jnp.int32)
    ends_float = pltpu.VMEM((blocks, per_block, width), jnp.float32)

    def flat(whole):
        return whole.reshape(rows, cols)

    def vmem(*arrays):
        return [pltpu.with_memory_space_constraint(array, pltpu.VMEM) for array in arrays]

    def exchange(values):
        return lax.all_to_all(values, AXES, split_axis=0, concat_axis=0, tiled=True)

    arguments = (
        end_device.T, end_local.T, trace_nodes, trace_weight, flat(aperture), flat(adj_source), flat(pressure)
    )
    message, aperture_here, source_here, pressure_here = pl.pallas_call(
        functools.partial(pack_kernel, grid_size * grid_size),
        out_shape=[pltpu.VMEM((device_count, 4, width), jnp.float32)] + [field] * 3,
        in_specs=[in_hbm] * 7,
        out_specs=[in_vmem] * 4,
        scratch_shapes=[
            pltpu.SMEM((2, owned_count), jnp.int32),
            pltpu.SMEM((2, owned_count), jnp.int32),
            pltpu.VMEM(trace_nodes.shape, jnp.int32),
            pltpu.VMEM(trace_weight.shape, jnp.float32),
            pltpu.SMEM((device_count,), jnp.int32),
            pltpu.SemaphoreType.DMA((4,)),
            pltpu.SemaphoreType.DMA((3,)),
        ],
        compiler_params=params,
        name="pack_ends",
    )(*[pltpu.with_memory_space_constraint(array, pltpu.HBM) for array in arguments])
    values_shape = pltpu.VMEM((device_count, 1, width), jnp.float32)
    values, row_hot, col_hot, col, weight, count, peer, parts, adjoint = pl.pallas_call(
        functools.partial(first_kernel, grid_size),
        out_shape=[
            values_shape,
            pltpu.VMEM((blocks, rows, per_block * width), jnp.bfloat16),
            pltpu.VMEM((blocks, cols, per_block * width), jnp.bfloat16),
            ends_int,
            ends_float,
            pltpu.VMEM((device_count, width), jnp.int32),
            ends_int,
            pltpu.VMEM((5, rows, cols), jnp.float32),
            field,
        ],
        in_specs=[in_vmem] * 3,
        out_specs=[in_vmem] * 9,
        scratch_shapes=[ends_int, field] + leaving,
        compiler_params=params,
        name="first_values",
    )(*vmem(exchange(message), aperture_here, source_here))
    for _ in range(SWEEPS - 1):
        values, adjoint = pl.pallas_call(
            sweep_kernel,
            out_shape=[values_shape, field],
            in_specs=[in_vmem] * 10,
            out_specs=[in_vmem] * 2,
            scratch_shapes=sweeping + leaving,
            compiler_params=params,
            name="sweep",
        )(
            *vmem(
                exchange(values), row_hot, col_hot, col, weight, count, peer, parts, adjoint, source_here
            )
        )
    gradient, adjoint = pl.pallas_call(
        functools.partial(last_kernel, grid_size),
        out_shape=[jax.ShapeDtypeStruct((rows, cols), jnp.float32)] * 2,
        in_specs=[in_vmem] * 11,
        out_specs=[in_hbm] * 2,
        scratch_shapes=sweeping
        + [pltpu.VMEM((4, rows, cols), jnp.float32), field, field, pltpu.SemaphoreType.DMA((2,))],
        compiler_params=params,
        name="last_sweep",
    )(
        *vmem(
            exchange(values), row_hot, col_hot, weight, count, peer, parts, adjoint,
            source_here, aperture_here, pressure_here,
        )
    )
    return gradient.reshape(aperture.shape), adjoint.reshape(aperture.shape)


def solution(mesh):
    fields, pairs = P(AXES, None, None), P(AXES, None)
    return jax.shard_map(
        body,
        mesh=mesh,
        in_specs=(fields, fields, fields, pairs, pairs, pairs, fields),
        out_specs=(fields, fields),
        check_vma=False,
    )
```

time: 51.2 us -> 50 us (0.977)
  Pallas kernels: 9.28 us -> 8.02 us
    pallas_call x2, Pallas kernels: 3.77 us -> 3.22 us  [body(): pl.pallas_call(sweep_kernel, out_shape=[values_shape, field], in_specs=[i...]
where the time goes in v4:
time: 50 us; the launch traced here: 49.7 us
  blocking collectives  41 us (82%)
  Pallas kernels  8.02 us (16%)
  between operations  0.65 us (1%)
    all_to_all x4, blocking collectives, exchange(): return lax.all_to_all(values, AXES, split_axis=0, concat_axis=0, tiled=True)  41 us
    pallas_call x2, Pallas kernels, body(): pl.pallas_call(sweep_kernel, out_shape=[values_shape, field], in_specs=[i...  3.22 us
    pallas_call x1, Pallas kernels, body(): pl.pallas_call(functools.partial(last_kernel, grid_size), out_shape=[jax....  1.87 us
    pallas_call x1, Pallas kernels, body(): pl.pallas_call(functools.partial(first_kernel, grid_size), out_shape=[val...  1.81 us
    pallas_call x1, Pallas kernels, body(): pl.pallas_call(functools.partial(pack_kernel, grid_size * grid_size), out...  1.13 us

profile of v4, /device:TPU:0, one launch (start us, length us, event | category | flops | bytes accessed | tf_op | source)
XLA Modules:
  0.0 49.7 jit_solution(6482440062034751582)
XLA Ops:
  0.6 1.1 %pack_ends.1 = (f32[32,4,128]{2,1,0:T(4,128)S(1)}, f32[256,128]{1,0:T(8,128)S(1)}, f32[256,128]{1,0:T(8,128)S(1)}, f32[256,128]{1,0:T(8,128)S(1)}) custom-call(s32[2,16]{1,0:T(2,128)} %bitcast.10, s32[2,16]{1,0:T(2,128)} %bitcast.11, s32[16,2,64]{2,1,0:T(2,128)} %nodes_hbm.1, f32[16,64]{1,0:T(8,128)} %weight_hbm.1, f32[256,128]{1,0:T(8,128)} %bitcast.7, ...), custom_call_target="tpu_custom_call" | custom-call | tf_op jit(solution)/shard_map/pack_ends/pallas_call | solution.py:376
  1.8 14.5 %all_to_all.20.message_ref = f32[32,4,128]{2,1,0:T(4,128)S(1)} all-to-all(f32[32,4,128]{2,1,0:T(4,128)S(1)} %get-tuple-element.21), channel_id=1, replica_groups=mesh['wide'=8,'narrow'=4] {'wide','narrow'}, dimensions={0} | all-to-all | bytes 131072 | tf_op jit(solution)/shard_map/all_to_all | solution.py:371
  16.3 1.8 %first_values.1 = (f32[32,1,128]{2,1,0:T(1,128)S(1)}, bf16[2,256,2048]{2,1,0:T(8,128)(2,1)S(1)}, bf16[2,128,2048]{2,1,0:T(8,128)(2,1)S(1)}, s32[2,16,128]{2,1,0:...) custom-call(f32[32,4,128]{2,1,0:T(4,128)S(1)} %all_to_all.20.message, ...), custom_call_target="tpu_custom_call" | custom-call | tf_op jit(solution)/shard_map/first_values/pallas_call | solution.py:394
  18.1 8.8 %all_to_all.21.arrived_ref = f32[32,1,128]{2,1,0:T(1,128)S(1)} all-to-all(f32[32,1,128]{2,1,0:T(1,128)S(1)} %get-tuple-element.24), channel_id=1, replica_groups=mesh['wide'=8,'narrow'=4] {'wide','narrow'}, dimensions={0} | all-to-all | bytes 32768 | tf_op jit(solution)/shard_map/all_to_all | solution.py:371
  26.9 1.6 %sweep.2 = (f32[32,1,128]{2,1,0:T(1,128)S(1)}, f32[256,128]{1,0:T(8,128)S(1)}) custom-call(f32[32,1,128]{2,1,0:T(1,128)S(1)} %all_to_all.21.arrived_ref, bf16[2,256,2048]{2,1,0:T(8,128)(2,1)S(1)} %get-tuple-element.25.row_hot_ref, bf16[2,128,2048]{2,1,0:T(8,128)(2,1)S(1)} %get-tuple-element.26.col_hot_ref, s32[2,16,128]{2,1,0:T(8,128)S(1)} %get-tuple-element.27.col_ref, ...), custom_call_target="tpu_custom_call" | custom-call | tf_op jit(solution)/shard_map/sweep/pallas_call | solution.py:414
  28.6 8.8 %all_to_all.22.arrived_ref = f32[32,1,128]{2,1,0:T(1,128)S(1)} all-to-all(f32[32,1,128]{2,1,0:T(1,128)S(1)} %get-tuple-element.33), channel_id=1, replica_groups=mesh['wide'=8,'narrow'=4] {'wide','narrow'}, dimensions={0} | all-to-all | bytes 32768 | tf_op jit(solution)/shard_map/all_to_all | solution.py:371
  37.4 1.6 %sweep.3 = (f32[32,1,128]{2,1,0:T(1,128)S(1)}, f32[256,128]{1,0:T(8,128)S(1)}) custom-call(f32[32,1,128]{2,1,0:T(1,128)S(1)} %all_to_all.22.arrived_ref, bf16[2,256,2048]{2,1,0:T(8,128)(2,1)S(1)} %get-tuple-element.25.row_hot_ref, bf16[2,128,2048]{2,1,0:T(8,128)(2,1)S(1)} %get-tuple-element.26.col_hot_ref, s32[2,16,128]{2,1,0:T(8,128)S(1)} %get-tuple-element.27.col_ref, ...), custom_call_target="tpu_custom_call" | custom-call | tf_op jit(solution)/shard_map/sweep/pallas_call | solution.py:414
  39.0 8.8 %all_to_all.23.arrived_ref = f32[32,1,128]{2,1,0:T(1,128)S(1)} all-to-all(f32[32,1,128]{2,1,0:T(1,128)S(1)} %get-tuple-element.35), channel_id=1, replica_groups=mesh['wide'=8,'narrow'=4] {'wide','narrow'}, dimensions={0} | all-to-all | bytes 32768 | tf_op jit(solution)/shard_map/all_to_all | solution.py:371
  47.9 1.9 %last_sweep.1 = (f32[256,128]{1,0:T(8,128)}, f32[256,128]{1,0:T(8,128)}) custom-call(f32[32,1,128]{2,1,0:T(1,128)S(1)} %all_to_all.23.arrived_ref, bf16[2,256,2048]{2,1,0:T(8,128)(2,1)S(1)} %get-tuple-element.25.row_hot_ref, bf16[2,128,2048]{2,1,0:T(8,128)(2,1)S(1)} %get-tuple-element.26.col_hot_ref, f32[2,16,128]{2,1,0:T(8,128)S(1)} %get-tuple-element.28.weight_ref, ...), custom_call_target="tpu_custom_call" | custom-call | tf_op jit(solution)/shard_map/last_sweep/pallas_call | solution.py:427

commit v5 on v4

--- a/solution.py
+++ b/solution.py
@@ -15,27 +15,28 @@
 SLICE = 8
 
 
+def start_copies(pairs, sems):
+    copies = [
+        pltpu.make_async_copy(source, target, sems.at[index]) for index, (source, target) in enumerate(pairs)
+    ]
+    for copy in copies:
+        copy.start()
+    return copies
+
+
 def pack_kernel(
-    cells_per, dest_hbm, local_hbm, nodes_hbm, weight_hbm, aperture_hbm, source_hbm, pressure_hbm,
-    out_ref, aperture_ref, source_ref, pressure_ref,
-    dest_ref, local_ref, nodes_ref, weight_ref, seen_ref, small_sems, large_sems,
+    cells_per, dest_hbm, local_hbm, nodes_hbm, weight_hbm, aperture_hbm,
+    out_ref, aperture_ref, dest_ref, local_ref, nodes_ref, weight_ref, seen_ref, sems,
 ):
     owned = nodes_ref.shape[0]
     devices, _, width = out_ref.shape
-    small = [
-        pltpu.make_async_copy(source, target, small_sems.at[index])
-        for index, (source, target) in enumerate(
-            ((dest_hbm, dest_ref), (local_hbm, local_ref), (nodes_hbm, nodes_ref), (weight_hbm, weight_ref))
-        )
-    ]
-    large = [
-        pltpu.make_async_copy(source, target, large_sems.at[index])
-        for index, (source, target) in enumerate(
-            ((aperture_hbm, aperture_ref), (source_hbm, source_ref), (pressure_hbm, pressure_ref))
-        )
-    ]
-    for copy in small + large:
-        copy.start()
+    copies = start_copies(
+        (
+            (dest_hbm, dest_ref), (local_hbm, local_ref), (nodes_hbm, nodes_ref), (weight_hbm, weight_ref),
+            (aperture_hbm, aperture_ref),
+        ),
+        sems,
+    )
 
     def clear(device, carry):
         seen_ref[device] = 0
@@ -44,7 +45,7 @@
     lax.fori_loop(0, devices, clear, 0, unroll=8)
     out_ref[:, 0:2, :] = jnp.zeros((devices, 2, width), jnp.float32)
     out_ref[:, 2:4, :] = jnp.full((devices, 2, width), -1.0, jnp.float32)
-    for copy in small:
+    for copy in copies[:4]:
         copy.wait()
 
     def place(index, carry):
@@ -63,8 +64,7 @@
         return carry
 
     lax.fori_loop(0, owned, place, 0, unroll=True)
-    for copy in large:
-        copy.wait()
+    copies[4].wait()
 
 
 def face_parts(conduct, grid_size):
@@ -161,14 +161,22 @@
 
 
 def first_kernel(
-    grid_size, message_ref, aperture_ref, source_ref,
+    grid_size, message_ref, aperture_ref, source_hbm, pressure_hbm,
     values_ref, row_hot_ref, col_hot_ref, col_ref, weight_ref, count_ref, peer_ref, parts_ref, adjoint_ref,
-    row_ref, total_ref, both_ref,
+    source_ref, pressure_ref, row_ref, total_ref, both_ref, sems,
 ):
+    copies = start_copies(
+        ((source_hbm, source_ref), (pressure_hbm, pressure_ref)), sems
+    )
     devices, _, width = message_ref.shape
     trace_len = width // 2
     blocks, per_block, _ = col_ref.shape
     rows, cols = aperture_ref.shape
+    aperture = aperture_ref[...]
+    faces = face_parts(aperture * aperture * aperture / 12.0, grid_size)
+    for index in range(4):
+        parts_ref[index] = faces[index]
+    parts_ref[4] = LEAKAGE + (faces[0] + faces[1] + faces[2] + faces[3])
     slots = [message_ref[:, rank, :] for rank in range(2)]
     partners = [message_ref[:, 2 + rank, :] for rank in range(2)]
     down = lax.broadcasted_iota(jnp.int32, (devices, width), 0)
@@ -225,11 +233,11 @@
         )
 
     over_blocks(count_ref, blocks, build)
-    aperture = aperture_ref[...]
-    faces = face_parts(aperture * aperture * aperture / 12.0, grid_size)
-    inv_diag = 1.0 / (LEAKAGE + (faces[0] + faces[1] + faces[2] + faces[3]) + total_ref[...])
+    inv_diag = 1.0 / (parts_ref[4] + total_ref[...])
+    for copy in copies:
+        copy.wait()
     for index in range(4):
-        parts_ref[index] = faces[index] * inv_diag
+        parts_ref[index] = parts_ref[index] * inv_diag
     parts_ref[4] = inv_diag
     adjoint = source_ref[...] * inv_diag
     adjoint_ref[...] = adjoint
@@ -367,31 +375,32 @@
     def vmem(*arrays):
         return [pltpu.with_memory_space_constraint(array, pltpu.VMEM) for array in arrays]
 
+    def hbm(*arrays):
+        return [pltpu.with_memory_space_constraint(array, pltpu.HBM) for array in arrays]
+
     def exchange(values):
         return lax.all_to_all(values, AXES, split_axis=0, concat_axis=0, tiled=True)
 
-    arguments = (
-        end_device.T, end_local.T, trace_nodes, trace_weight, flat(aperture), flat(adj_source), flat(pressure)
-    )
-    message, aperture_here, source_here, pressure_here = pl.pallas_call(
+    message, aperture_here = pl.pallas_call(
         functools.partial(pack_kernel, grid_size * grid_size),
-        out_shape=[pltpu.VMEM((device_count, 4, width), jnp.float32)] + [field] * 3,
-        in_specs=[in_hbm] * 7,
-        out_specs=[in_vmem] * 4,
+        out_shape=[pltpu.VMEM((device_count, 4, width), jnp.float32), field],
+        in_specs=[in_hbm] * 5,
+        out_specs=[in_vmem] * 2,
         scratch_shapes=[
             pltpu.SMEM((2, owned_count), jnp.int32),
             pltpu.SMEM((2, owned_count), jnp.int32),
             pltpu.VMEM(trace_nodes.shape, jnp.int32),
             pltpu.VMEM(trace_weight.shape, jnp.float32),
             pltpu.SMEM((device_count,), jnp.int32),
-            pltpu.SemaphoreType.DMA((4,)),
-            pltpu.SemaphoreType.DMA((3,)),
+            pltpu.SemaphoreType.DMA((5,)),
         ],
         compiler_params=params,
         name="pack_ends",
-    )(*[pltpu.with_memory_space_constraint(array, pltpu.HBM) for array in arguments])
+    )(*hbm(end_device.T, end_local.T, trace_nodes, trace_weight, flat(aperture)))
     values_shape = pltpu.VMEM((device_count, 1, width), jnp.float32)
-    values, row_hot, col_hot, col, weight, count, peer, parts, adjoint = pl.pallas_call(
+    (
+        values, row_hot, col_hot, col, weight, count, peer, parts, adjoint, source_here, pressure_here,
+    ) = pl.pallas_call(
         functools.partial(first_kernel, grid_size),
         out_shape=[
             values_shape,
@@ -402,14 +411,14 @@
             pltpu.VMEM((device_count, width), jnp.int32),
             ends_int,
             pltpu.VMEM((5, rows, cols), jnp.float32),
-            field,
-        ],
-        in_specs=[in_vmem] * 3,
-        out_specs=[in_vmem] * 9,
-        scratch_shapes=[ends_int, field] + leaving,
+        ]
+        + [field] * 3,
+        in_specs=[in_vmem] * 2 + [in_hbm] * 2,
+        out_specs=[in_vmem] * 11,
+        scratch_shapes=[ends_int, field] + leaving + [pltpu.SemaphoreType.DMA((2,))],
         compiler_params=params,
         name="first_values",
-    )(*vmem(exchange(message), aperture_here, source_here))
+    )(*vmem(exchange(message), aperture_here), *hbm(flat(adj_source), flat(pressure)))
     for _ in range(SWEEPS - 1):
         values, adjoint = pl.pallas_call(
             sweep_kernel,

time: 50 us -> 49.8 us (level)
  no operation moved by 1% of the time
where the time goes in v5:
time: 49.8 us; the launch traced here: 49.6 us
  blocking collectives  41 us (82%)
  Pallas kernels  7.88 us (16%)
  between operations  0.66 us (1%)
    all_to_all x4, blocking collectives, exchange(): return lax.all_to_all(values, AXES, split_axis=0, concat_axis=0, tiled=True)  41 us
    pallas_call x2, Pallas kernels, body(): pl.pallas_call(sweep_kernel, out_shape=[values_shape, field], in_specs=[i...  3.22 us
    pallas_call x1, Pallas kernels, body(): pl.pallas_call(functools.partial(last_kernel, grid_size), out_shape=[jax....  1.87 us
    pallas_call x1, Pallas kernels, body(): pl.pallas_call(functools.partial(first_kernel, grid_size), out_shape=[val...  1.81 us

profile of v5, /device:TPU:0, one launch (start us, length us, event | category | flops | bytes accessed | tf_op | source)
XLA Modules:
  0.0 49.6 jit_solution(4288974464866605336)
XLA Ops:
  0.6 1.0 %pack_ends.1 = (f32[32,4,128]{2,1,0:T(4,128)S(1)}, f32[256,128]{1,0:T(8,128)S(1)}) custom-call(s32[2,16]{1,0:T(2,128)} %bitcast.10, s32[2,16]{1,0:T(2,128)} %bitcast.11, s32[16,2,64]{2,1,0:T(2,128)} %nodes_hbm.1, f32[16,64]{1,0:T(8,128)} %weight_hbm.1, f32[256,128]{1,0:T(8,128)} %bitcast.9), custom_call_target="tpu_custom_call" | custom-call | tf_op jit(solution)/shard_map/pack_ends/pallas_call | solution.py:384
  1.6 14.5 %all_to_all.20.message_ref = f32[32,4,128]{2,1,0:T(4,128)S(1)} all-to-all(f32[32,4,128]{2,1,0:T(4,128)S(1)} %get-tuple-element.21), channel_id=1, replica_groups=mesh['wide'=8,'narrow'=4] {'wide','narrow'}, dimensions={0} | all-to-all | bytes 131072 | tf_op jit(solution)/shard_map/all_to_all | solution.py:382
  16.1 1.8 %first_values.1 = (f32[32,1,128]{2,1,0:T(1,128)S(1)}, bf16[2,256,2048]{2,1,0:T(8,128)(2,1)S(1)}, bf16[2,128,2048]{2,1,0:T(8,128)(2,1)S(1)}, s32[2,16,128]{2,1,0:...) custom-call(f32[32,4,128]{2,1,0:T(4,128)S(1)} %all_to_all.20.message, ...), custom_call_target="tpu_custom_call" | custom-call | tf_op jit(solution)/shard_map/first_values/pallas_call | solution.py:403
  18.0 8.8 %all_to_all.21.arrived_ref = f32[32,1,128]{2,1,0:T(1,128)S(1)} all-to-all(f32[32,1,128]{2,1,0:T(1,128)S(1)} %get-tuple-element.23), channel_id=1, replica_groups=mesh['wide'=8,'narrow'=4] {'wide','narrow'}, dimensions={0} | all-to-all | bytes 32768 | tf_op jit(solution)/shard_map/all_to_all | solution.py:382
  26.8 1.6 %sweep.2 = (f32[32,1,128]{2,1,0:T(1,128)S(1)}, f32[256,128]{1,0:T(8,128)S(1)}) custom-call(f32[32,1,128]{2,1,0:T(1,128)S(1)} %all_to_all.21.arrived_ref, bf16[2,256,2048]{2,1,0:T(8,128)(2,1)S(1)} %get-tuple-element.24.row_hot_ref, bf16[2,128,2048]{2,1,0:T(8,128)(2,1)S(1)} %get-tuple-element.25.col_hot_ref, s32[2,16,128]{2,1,0:T(8,128)S(1)} %get-tuple-element.26.col_ref, ...), custom_call_target="tpu_custom_call" | custom-call | tf_op jit(solution)/shard_map/sweep/pallas_call | solution.py:423
  28.4 8.8 %all_to_all.22.arrived_ref = f32[32,1,128]{2,1,0:T(1,128)S(1)} all-to-all(f32[32,1,128]{2,1,0:T(1,128)S(1)} %get-tuple-element.33), channel_id=1, replica_groups=mesh['wide'=8,'narrow'=4] {'wide','narrow'}, dimensions={0} | all-to-all | bytes 32768 | tf_op jit(solution)/shard_map/all_to_all | solution.py:382
  37.3 1.6 %sweep.3 = (f32[32,1,128]{2,1,0:T(1,128)S(1)}, f32[256,128]{1,0:T(8,128)S(1)}) custom-call(f32[32,1,128]{2,1,0:T(1,128)S(1)} %all_to_all.22.arrived_ref, bf16[2,256,2048]{2,1,0:T(8,128)(2,1)S(1)} %get-tuple-element.24.row_hot_ref, bf16[2,128,2048]{2,1,0:T(8,128)(2,1)S(1)} %get-tuple-element.25.col_hot_ref, s32[2,16,128]{2,1,0:T(8,128)S(1)} %get-tuple-element.26.col_ref, ...), custom_call_target="tpu_custom_call" | custom-call | tf_op jit(solution)/shard_map/sweep/pallas_call | solution.py:423
  38.9 8.8 %all_to_all.23.arrived_ref = f32[32,1,128]{2,1,0:T(1,128)S(1)} all-to-all(f32[32,1,128]{2,1,0:T(1,128)S(1)} %get-tuple-element.35), channel_id=1, replica_groups=mesh['wide'=8,'narrow'=4] {'wide','narrow'}, dimensions={0} | all-to-all | bytes 32768 | tf_op jit(solution)/shard_map/all_to_all | solution.py:382
  47.7 1.9 %last_sweep.1 = (f32[256,128]{1,0:T(8,128)}, f32[256,128]{1,0:T(8,128)}) custom-call(f32[32,1,128]{2,1,0:T(1,128)S(1)} %all_to_all.23.arrived_ref, bf16[2,256,2048]{2,1,0:T(8,128)(2,1)S(1)} %get-tuple-element.24.row_hot_ref, bf16[2,128,2048]{2,1,0:T(8,128)(2,1)S(1)} %get-tuple-element.25.col_hot_ref, f32[2,16,128]{2,1,0:T(8,128)S(1)} %get-tuple-element.27.weight_ref, ...), custom_call_target="tpu_custom_call" | custom-call | tf_op jit(solution)/shard_map/last_sweep/pallas_call | solution.py:436

commit v6 on v5

--- a/solution.py
+++ b/solution.py
@@ -30,10 +30,14 @@
 ):
     owned = nodes_ref.shape[0]
     devices, _, width = out_ref.shape
+    rows = aperture_ref.shape[0]
     copies = start_copies(
         (
             (dest_hbm, dest_ref), (local_hbm, local_ref), (nodes_hbm, nodes_ref), (weight_hbm, weight_ref),
-            (aperture_hbm, aperture_ref),
+        )
+        + tuple(
+            (aperture_hbm.at[pl.ds(first, rows // 4)], aperture_ref.at[pl.ds(first, rows // 4)])
+            for first in range(0, rows, rows // 4)
         ),
         sems,
     )
@@ -64,7 +68,8 @@
         return carry
 
     lax.fori_loop(0, owned, place, 0, unroll=True)
-    copies[4].wait()
+    for copy in copies[4:]:
+        copy.wait()
 
 
 def face_parts(conduct, grid_size):
@@ -236,8 +241,6 @@
     inv_diag = 1.0 / (parts_ref[4] + total_ref[...])
     for copy in copies:
         copy.wait()
-    for index in range(4):
-        parts_ref[index] = parts_ref[index] * inv_diag
     parts_ref[4] = inv_diag
     adjoint = source_ref[...] * inv_diag
     adjoint_ref[...] = adjoint
@@ -292,11 +295,11 @@
         for first in slices:
             here = slice(first, first + SLICE)
             if step == 0:
-                forcing = (source_ref[here] + total_ref[here]) * parts_ref[4, here]
+                forcing = source_ref[here] + total_ref[here]
                 total_ref[here] = forcing
-                now = forcing + early_ref[here]
+                now = (forcing + early_ref[here]) * parts_ref[4, here]
             else:
-                now = total_ref[here] + pull(old, first)
+                now = (total_ref[here] + pull(old, first)) * parts_ref[4, here]
             new[SLICE + first : 2 * SLICE + first] = now
             if step == INNER - 1:
                 adjoint_ref[here] = now
@@ -392,7 +395,7 @@
             pltpu.VMEM(trace_nodes.shape, jnp.int32),
             pltpu.VMEM(trace_weight.shape, jnp.float32),
             pltpu.SMEM((device_count,), jnp.int32),
-            pltpu.SemaphoreType.DMA((5,)),
+            pltpu.SemaphoreType.DMA((8,)),
         ],
         compiler_params=params,
         name="pack_ends",

time: 49.8 us -> 49.8 us (level)
  no operation moved by 1% of the time
where the time goes in v6:
time: 49.8 us; the launch traced here: 49.5 us
  blocking collectives  41 us (82%)
  Pallas kernels  7.82 us (16%)
  between operations  0.66 us (1%)
    all_to_all x4, blocking collectives, exchange(): return lax.all_to_all(values, AXES, split_axis=0, concat_axis=0, tiled=True)  41 us
    pallas_call x2, Pallas kernels, body(): pl.pallas_call(sweep_kernel, out_shape=[values_shape, field], in_specs=[i...  3.23 us
    pallas_call x1, Pallas kernels, body(): pl.pallas_call(functools.partial(last_kernel, grid_size), out_shape=[jax....  1.87 us
    pallas_call x1, Pallas kernels, body(): pl.pallas_call(functools.partial(first_kernel, grid_size), out_shape=[val...  1.77 us

profile of v6, /device:TPU:0, one launch (start us, length us, event | category | flops | bytes accessed | tf_op | source)
XLA Modules:
  0.0 49.5 jit_solution(5979567995020835587)
XLA Ops:
  0.6 0.9 %pack_ends.1 = (f32[32,4,128]{2,1,0:T(4,128)S(1)}, f32[256,128]{1,0:T(8,128)S(1)}) custom-call(s32[2,16]{1,0:T(2,128)} %bitcast.10, s32[2,16]{1,0:T(2,128)} %bitcast.11, s32[16,2,64]{2,1,0:T(2,128)} %nodes_hbm.1, f32[16,64]{1,0:T(8,128)} %weight_hbm.1, f32[256,128]{1,0:T(8,128)} %bitcast.9), custom_call_target="tpu_custom_call" | custom-call | tf_op jit(solution)/shard_map/pack_ends/pallas_call | solution.py:387
  1.6 14.5 %all_to_all.20.message_ref = f32[32,4,128]{2,1,0:T(4,128)S(1)} all-to-all(f32[32,4,128]{2,1,0:T(4,128)S(1)} %get-tuple-element.21), channel_id=1, replica_groups=mesh['wide'=8,'narrow'=4] {'wide','narrow'}, dimensions={0} | all-to-all | bytes 131072 | tf_op jit(solution)/shard_map/all_to_all | solution.py:385
  16.1 1.8 %first_values.1 = (f32[32,1,128]{2,1,0:T(1,128)S(1)}, bf16[2,256,2048]{2,1,0:T(8,128)(2,1)S(1)}, bf16[2,128,2048]{2,1,0:T(8,128)(2,1)S(1)}, s32[2,16,128]{2,1,0:...) custom-call(f32[32,4,128]{2,1,0:T(4,128)S(1)} %all_to_all.20.message, ...), custom_call_target="tpu_custom_call" | custom-call | tf_op jit(solution)/shard_map/first_values/pallas_call | solution.py:406
  17.9 8.8 %all_to_all.21.arrived_ref = f32[32,1,128]{2,1,0:T(1,128)S(1)} all-to-all(f32[32,1,128]{2,1,0:T(1,128)S(1)} %get-tuple-element.23), channel_id=1, replica_groups=mesh['wide'=8,'narrow'=4] {'wide','narrow'}, dimensions={0} | all-to-all | bytes 32768 | tf_op jit(solution)/shard_map/all_to_all | solution.py:385
  26.7 1.6 %sweep.2 = (f32[32,1,128]{2,1,0:T(1,128)S(1)}, f32[256,128]{1,0:T(8,128)S(1)}) custom-call(f32[32,1,128]{2,1,0:T(1,128)S(1)} %all_to_all.21.arrived_ref, bf16[2,256,2048]{2,1,0:T(8,128)(2,1)S(1)} %get-tuple-element.24.row_hot_ref, bf16[2,128,2048]{2,1,0:T(8,128)(2,1)S(1)} %get-tuple-element.25.col_hot_ref, s32[2,16,128]{2,1,0:T(8,128)S(1)} %get-tuple-element.26.col_ref, ...), custom_call_target="tpu_custom_call" | custom-call | tf_op jit(solution)/shard_map/sweep/pallas_call | solution.py:426
  28.3 8.8 %all_to_all.22.arrived_ref = f32[32,1,128]{2,1,0:T(1,128)S(1)} all-to-all(f32[32,1,128]{2,1,0:T(1,128)S(1)} %get-tuple-element.33), channel_id=1, replica_groups=mesh['wide'=8,'narrow'=4] {'wide','narrow'}, dimensions={0} | all-to-all | bytes 32768 | tf_op jit(solution)/shard_map/all_to_all | solution.py:385
  37.2 1.6 %sweep.3 = (f32[32,1,128]{2,1,0:T(1,128)S(1)}, f32[256,128]{1,0:T(8,128)S(1)}) custom-call(f32[32,1,128]{2,1,0:T(1,128)S(1)} %all_to_all.22.arrived_ref, bf16[2,256,2048]{2,1,0:T(8,128)(2,1)S(1)} %get-tuple-element.24.row_hot_ref, bf16[2,128,2048]{2,1,0:T(8,128)(2,1)S(1)} %get-tuple-element.25.col_hot_ref, s32[2,16,128]{2,1,0:T(8,128)S(1)} %get-tuple-element.26.col_ref, ...), custom_call_target="tpu_custom_call" | custom-call | tf_op jit(solution)/shard_map/sweep/pallas_call | solution.py:426
  38.8 8.8 %all_to_all.23.arrived_ref = f32[32,1,128]{2,1,0:T(1,128)S(1)} all-to-all(f32[32,1,128]{2,1,0:T(1,128)S(1)} %get-tuple-element.35), channel_id=1, replica_groups=mesh['wide'=8,'narrow'=4] {'wide','narrow'}, dimensions={0} | all-to-all | bytes 32768 | tf_op jit(solution)/shard_map/all_to_all | solution.py:385
  47.7 1.9 %last_sweep.1 = (f32[256,128]{1,0:T(8,128)}, f32[256,128]{1,0:T(8,128)}) custom-call(f32[32,1,128]{2,1,0:T(1,128)S(1)} %all_to_all.23.arrived_ref, bf16[2,256,2048]{2,1,0:T(8,128)(2,1)S(1)} %get-tuple-element.24.row_hot_ref, bf16[2,128,2048]{2,1,0:T(8,128)(2,1)S(1)} %get-tuple-element.25.col_hot_ref, f32[2,16,128]{2,1,0:T(8,128)S(1)} %get-tuple-element.27.weight_ref, ...), custom_call_target="tpu_custom_call" | custom-call | tf_op jit(solution)/shard_map/last_sweep/pallas_call | solution.py:439

commit v7 on v6

--- a/solution.py
+++ b/solution.py
@@ -134,41 +134,37 @@
         total_ref[...] += total
 
 
-def gather(row_hot_ref, col_ref, peer_ref, both_ref, values_ref, block):
-    _, per_block, width = col_ref.shape
-    cols = both_ref.shape[0] // 2
+def gather(col_hot_ref, row_ref, peer_ref, both_ref, values_ref, block):
+    _, per_block, width = row_ref.shape
+    rows = both_ref.shape[0]
     group = 2
-    col_ids = lax.broadcasted_iota(jnp.int32, (cols, width), 0)
+    row_ids = lax.broadcasted_iota(jnp.int32, (rows, width), 0)
     both = both_ref[...]
     for start in range(0, per_block, group):
-        picked = jnp.dot(
-            both,
-            row_hot_ref[block, :, start * width : (start + group) * width],
-            preferred_element_type=jnp.float32,
-        )
-        picked = picked[:cols] + picked[cols:]
+        hot = col_hot_ref[block, :, start * width : (start + group) * width]
+        picked = jnp.dot(both, jnp.concatenate([hot, hot], axis=0), preferred_element_type=jnp.float32)
         for offset in range(group):
             device = start + offset
             mine = picked[:, offset * width : (offset + 1) * width]
-            hit = col_ids == col_ref[block, device : device + 1, :]
+            hit = row_ids == row_ref[block, device : device + 1, :]
             values_ref[peer_ref[block, device, 0]] = jnp.sum(
                 jnp.where(hit, mine, 0.0), axis=0, keepdims=True
             )
 
 
-def send_values(adjoint, row_hot_ref, col_ref, count_ref, peer_ref, both_ref, values_ref):
+def send_values(adjoint, col_hot_ref, row_ref, count_ref, peer_ref, both_ref, values_ref):
     values_ref[...] = jnp.zeros(values_ref.shape, jnp.float32)
-    both_ref[...] = jnp.concatenate(split_pair(adjoint.T), axis=0)
+    both_ref[...] = jnp.concatenate(split_pair(adjoint), axis=1)
     over_blocks(
-        count_ref, col_ref.shape[0],
-        lambda block: gather(row_hot_ref, col_ref, peer_ref, both_ref, values_ref, block),
+        count_ref, row_ref.shape[0],
+        lambda block: gather(col_hot_ref, row_ref, peer_ref, both_ref, values_ref, block),
     )
 
 
 def first_kernel(
     grid_size, message_ref, aperture_ref, source_hbm, pressure_hbm,
-    values_ref, row_hot_ref, col_hot_ref, col_ref, weight_ref, count_ref, peer_ref, parts_ref, adjoint_ref,
-    source_ref, pressure_ref, row_ref, total_ref, both_ref, sems,
+    values_ref, row_hot_ref, col_hot_ref, row_ref, weight_ref, count_ref, peer_ref, parts_ref, adjoint_ref,
+    source_ref, pressure_ref, col_ref, total_ref, both_ref, sems,
 ):
     copies = start_copies(
         ((source_hbm, source_ref), (pressure_hbm, pressure_ref)), sems
@@ -244,7 +240,7 @@
     parts_ref[4] = inv_diag
     adjoint = source_ref[...] * inv_diag
     adjoint_ref[...] = adjoint
-    send_values(adjoint, row_hot_ref, col_ref, count_ref, peer_ref, both_ref, values_ref)
+    send_values(adjoint, col_hot_ref, row_ref, count_ref, peer_ref, both_ref, values_ref)
 
 
 def near(state_ref, rows):
@@ -306,14 +302,14 @@
 
 
 def sweep_kernel(
-    arrived_ref, row_hot_ref, col_hot_ref, col_ref, weight_ref, count_ref, peer_ref, parts_ref, start_ref,
+    arrived_ref, row_hot_ref, col_hot_ref, row_ref, weight_ref, count_ref, peer_ref, parts_ref, start_ref,
     source_ref, values_ref, adjoint_ref, total_ref, early_ref, state_ref, both_ref,
 ):
     relax(
         arrived_ref, row_hot_ref, col_hot_ref, weight_ref, count_ref, peer_ref, parts_ref, start_ref, source_ref,
         adjoint_ref, total_ref, early_ref, state_ref,
     )
-    send_values(adjoint_ref[...], row_hot_ref, col_ref, count_ref, peer_ref, both_ref, values_ref)
+    send_values(adjoint_ref[...], col_hot_ref, row_ref, count_ref, peer_ref, both_ref, values_ref)
 
 
 def last_kernel(
@@ -368,7 +364,7 @@
     params = pltpu.CompilerParams(vmem_limit_bytes=(8 << 20) + nodes * 1024)
     field = pltpu.VMEM((rows, cols), jnp.float32)
     sweeping = [field, field, pltpu.VMEM((2, rows + 2 * SLICE, cols), jnp.float32)]
-    leaving = [pltpu.VMEM((2 * cols, rows), jnp.bfloat16)]
+    leaving = [pltpu.VMEM((rows, 2 * cols), jnp.bfloat16)]
     ends_int = pltpu.VMEM((blocks, per_block, width), jnp.int32)
     ends_float = pltpu.VMEM((blocks, per_block, width), jnp.float32)
 
@@ -402,7 +398,7 @@
     )(*hbm(end_device.T, end_local.T, trace_nodes, trace_weight, flat(aperture)))
     values_shape = pltpu.VMEM((device_count, 1, width), jnp.float32)
     (
-        values, row_hot, col_hot, col, weight, count, peer, parts, adjoint, source_here, pressure_here,
+        values, row_hot, col_hot, row, weight, count, peer, parts, adjoint, source_here, pressure_here,
     ) = pl.pallas_call(
         functools.partial(first_kernel, grid_size),
         out_shape=[
@@ -433,7 +429,7 @@
             name="sweep",
         )(
             *vmem(
-                exchange(values), row_hot, col_hot, col, weight, count, peer, parts, adjoint, source_here
+                exchange(values), row_hot, col_hot, row, weight, count, peer, parts, adjoint, source_here
             )
         )
     gradient, adjoint = pl.pallas_call(

time: 49.8 us -> 49.7 us (level)
  no operation moved by 1% of the time
where the time goes in v7:
time: 49.7 us; the launch traced here: 49.4 us
  blocking collectives  41 us (82%)
  Pallas kernels  7.72 us (16%)
  between operations  0.66 us (1%)
    all_to_all x4, blocking collectives, exchange(): return lax.all_to_all(values, AXES, split_axis=0, concat_axis=0, tiled=True)  41 us
    pallas_call x2, Pallas kernels, body(): pl.pallas_call(sweep_kernel, out_shape=[values_shape, field], in_specs=[i...  3.11 us
    pallas_call x1, Pallas kernels, body(): pl.pallas_call(functools.partial(last_kernel, grid_size), out_shape=[jax....  1.87 us
    pallas_call x1, Pallas kernels, body(): pl.pallas_call(functools.partial(first_kernel, grid_size), out_shape=[val...  1.78 us

profile of v7, /device:TPU:0, one launch (start us, length us, event | category | flops | bytes accessed | tf_op | source)
XLA Modules:
  0.0 49.4 jit_solution(3300071214589810752)
XLA Ops:
  0.6 0.9 %pack_ends.1 = (f32[32,4,128]{2,1,0:T(4,128)S(1)}, f32[256,128]{1,0:T(8,128)S(1)}) custom-call(s32[2,16]{1,0:T(2,128)} %bitcast.10, s32[2,16]{1,0:T(2,128)} %bitcast.11, s32[16,2,64]{2,1,0:T(2,128)} %nodes_hbm.1, f32[16,64]{1,0:T(8,128)} %weight_hbm.1, f32[256,128]{1,0:T(8,128)} %bitcast.9), custom_call_target="tpu_custom_call" | custom-call | tf_op jit(solution)/shard_map/pack_ends/pallas_call | solution.py:383
  1.6 14.5 %all_to_all.20.message_ref = f32[32,4,128]{2,1,0:T(4,128)S(1)} all-to-all(f32[32,4,128]{2,1,0:T(4,128)S(1)} %get-tuple-element.21), channel_id=1, replica_groups=mesh['wide'=8,'narrow'=4] {'wide','narrow'}, dimensions={0} | all-to-all | bytes 131072 | tf_op jit(solution)/shard_map/all_to_all | solution.py:381
  16.1 1.8 %first_values.1 = (f32[32,1,128]{2,1,0:T(1,128)S(1)}, bf16[2,256,2048]{2,1,0:T(8,128)(2,1)S(1)}, bf16[2,128,2048]{2,1,0:T(8,128)(2,1)S(1)}, s32[2,16,128]{2,1,0:...) custom-call(f32[32,4,128]{2,1,0:T(4,128)S(1)} %all_to_all.20.message, ...), custom_call_target="tpu_custom_call" | custom-call | tf_op jit(solution)/shard_map/first_values/pallas_call | solution.py:402
  17.9 8.8 %all_to_all.21.arrived_ref = f32[32,1,128]{2,1,0:T(1,128)S(1)} all-to-all(f32[32,1,128]{2,1,0:T(1,128)S(1)} %get-tuple-element.23), channel_id=1, replica_groups=mesh['wide'=8,'narrow'=4] {'wide','narrow'}, dimensions={0} | all-to-all | bytes 32768 | tf_op jit(solution)/shard_map/all_to_all | solution.py:381
  26.7 1.6 %sweep.2 = (f32[32,1,128]{2,1,0:T(1,128)S(1)}, f32[256,128]{1,0:T(8,128)S(1)}) custom-call(f32[32,1,128]{2,1,0:T(1,128)S(1)} %all_to_all.21.arrived_ref, bf16[2,256,2048]{2,1,0:T(8,128)(2,1)S(1)} %get-tuple-element.24.row_hot_ref, bf16[2,128,2048]{2,1,0:T(8,128)(2,1)S(1)} %get-tuple-element.25.col_hot_ref, s32[2,16,128]{2,1,0:T(8,128)S(1)} %get-tuple-element.26.row_ref, ...), custom_call_target="tpu_custom_call" | custom-call | tf_op jit(solution)/shard_map/sweep/pallas_call | solution.py:422
  28.3 8.8 %all_to_all.22.arrived_ref = f32[32,1,128]{2,1,0:T(1,128)S(1)} all-to-all(f32[32,1,128]{2,1,0:T(1,128)S(1)} %get-tuple-element.33), channel_id=1, replica_groups=mesh['wide'=8,'narrow'=4] {'wide','narrow'}, dimensions={0} | all-to-all | bytes 32768 | tf_op jit(solution)/shard_map/all_to_all | solution.py:381
  37.1 1.6 %sweep.3 = (f32[32,1,128]{2,1,0:T(1,128)S(1)}, f32[256,128]{1,0:T(8,128)S(1)}) custom-call(f32[32,1,128]{2,1,0:T(1,128)S(1)} %all_to_all.22.arrived_ref, bf16[2,256,2048]{2,1,0:T(8,128)(2,1)S(1)} %get-tuple-element.24.row_hot_ref, bf16[2,128,2048]{2,1,0:T(8,128)(2,1)S(1)} %get-tuple-element.25.col_hot_ref, s32[2,16,128]{2,1,0:T(8,128)S(1)} %get-tuple-element.26.row_ref, ...), custom_call_target="tpu_custom_call" | custom-call | tf_op jit(solution)/shard_map/sweep/pallas_call | solution.py:422
  38.7 8.8 %all_to_all.23.arrived_ref = f32[32,1,128]{2,1,0:T(1,128)S(1)} all-to-all(f32[32,1,128]{2,1,0:T(1,128)S(1)} %get-tuple-element.35), channel_id=1, replica_groups=mesh['wide'=8,'narrow'=4] {'wide','narrow'}, dimensions={0} | all-to-all | bytes 32768 | tf_op jit(solution)/shard_map/all_to_all | solution.py:381
  47.6 1.9 %last_sweep.1 = (f32[256,128]{1,0:T(8,128)}, f32[256,128]{1,0:T(8,128)}) custom-call(f32[32,1,128]{2,1,0:T(1,128)S(1)} %all_to_all.23.arrived_ref, bf16[2,256,2048]{2,1,0:T(8,128)(2,1)S(1)} %get-tuple-element.24.row_hot_ref, bf16[2,128,2048]{2,1,0:T(8,128)(2,1)S(1)} %get-tuple-element.25.col_hot_ref, f32[2,16,128]{2,1,0:T(8,128)S(1)} %get-tuple-element.27.weight_ref, ...), custom_call_target="tpu_custom_call" | custom-call | tf_op jit(solution)/shard_map/last_sweep/pallas_call | solution.py:435

commit v8 on v7

--- a/solution.py
+++ b/solution.py
@@ -257,7 +257,7 @@
 
 def relax(
     arrived_ref, row_hot_ref, col_hot_ref, weight_ref, count_ref, peer_ref, parts_ref, start_ref, source_ref,
-    adjoint_ref, total_ref, early_ref, state_ref, before_ref=None,
+    adjoint_ref, total_ref, early_ref, state_ref, scaled_ref, before_ref=None,
 ):
     rows, cols = start_ref.shape
     slices = range(0, rows, SLICE)
@@ -270,10 +270,12 @@
     def pull(state, first):
         _, (below, above, right, left) = near(state, first)
         here = slice(first, first + SLICE)
-        return (parts_ref[0, here] * below + parts_ref[1, here] * above) + (
-            parts_ref[2, here] * right + parts_ref[3, here] * left
-        )
-
+        return (scaled_ref[0, here] * below + scaled_ref[1, here] * above) + (
+            scaled_ref[2, here] * right + scaled_ref[3, here] * left
+        )
+
+    for index in range(4):
+        scaled_ref[index] = parts_ref[index] * parts_ref[4]
     for first in slices:
         early_ref[first : first + SLICE] = pull(state_ref.at[0], first)
     if before_ref is not None:
@@ -291,11 +293,11 @@
         for first in slices:
             here = slice(first, first + SLICE)
             if step == 0:
-                forcing = source_ref[here] + total_ref[here]
+                forcing = (source_ref[here] + total_ref[here]) * parts_ref[4, here]
                 total_ref[here] = forcing
-                now = (forcing + early_ref[here]) * parts_ref[4, here]
+                now = forcing + early_ref[here]
             else:
-                now = (total_ref[here] + pull(old, first)) * parts_ref[4, here]
+                now = total_ref[here] + pull(old, first)
             new[SLICE + first : 2 * SLICE + first] = now
             if step == INNER - 1:
                 adjoint_ref[here] = now
@@ -303,11 +305,11 @@
 
 def sweep_kernel(
     arrived_ref, row_hot_ref, col_hot_ref, row_ref, weight_ref, count_ref, peer_ref, parts_ref, start_ref,
-    source_ref, values_ref, adjoint_ref, total_ref, early_ref, state_ref, both_ref,
+    source_ref, values_ref, adjoint_ref, total_ref, early_ref, state_ref, scaled_ref, both_ref,
 ):
     relax(
         arrived_ref, row_hot_ref, col_hot_ref, weight_ref, count_ref, peer_ref, parts_ref, start_ref, source_ref,
-        adjoint_ref, total_ref, early_ref, state_ref,
+        adjoint_ref, total_ref, early_ref, state_ref, scaled_ref,
     )
     send_values(adjoint_ref[...], col_hot_ref, row_ref, count_ref, peer_ref, both_ref, values_ref)
 
@@ -315,7 +317,7 @@
 def last_kernel(
     grid_size, arrived_ref, row_hot_ref, col_hot_ref, weight_ref, count_ref, peer_ref, parts_ref, start_ref,
     source_ref, aperture_ref, pressure_ref, gradient_hbm, adjoint_hbm,
-    total_ref, early_ref, state_ref, share_ref, gradient_ref, adjoint_ref, sems,
+    total_ref, early_ref, state_ref, scaled_ref, share_ref, gradient_ref, adjoint_ref, sems,
 ):
     rows, cols = start_ref.shape
     slices = range(0, rows, SLICE)
@@ -335,7 +337,7 @@
 
     relax(
         arrived_ref, row_hot_ref, col_hot_ref, weight_ref, count_ref, peer_ref, parts_ref, start_ref, source_ref,
-        adjoint_ref, total_ref, early_ref, state_ref, shares,
+        adjoint_ref, total_ref, early_ref, state_ref, scaled_ref, shares,
     )
     keep = pltpu.make_async_copy(adjoint_ref, adjoint_hbm, sems.at[0])
     keep.start()
@@ -363,7 +365,8 @@
     in_hbm = pl.BlockSpec(memory_space=pltpu.HBM)
     params = pltpu.CompilerParams(vmem_limit_bytes=(8 << 20) + nodes * 1024)
     field = pltpu.VMEM((rows, cols), jnp.float32)
-    sweeping = [field, field, pltpu.VMEM((2, rows + 2 * SLICE, cols), jnp.float32)]
+    four = pltpu.VMEM((4, rows, cols), jnp.float32)
+    sweeping = [field, field, pltpu.VMEM((2, rows + 2 * SLICE, cols), jnp.float32), four]
     leaving = [pltpu.VMEM((rows, 2 * cols), jnp.bfloat16)]
     ends_int = pltpu.VMEM((blocks, per_block, width), jnp.int32)
     ends_float = pltpu.VMEM((blocks, per_block, width), jnp.float32)

time: 49.7 us -> 49.7 us (level)
  no operation moved by 1% of the time
where the time goes in v8:
time: 49.7 us; the launch traced here: 49.4 us
  blocking collectives  41 us (82%)
  Pallas kernels  7.72 us (16%)
  between operations  0.66 us (1%)
    all_to_all x4, blocking collectives, exchange(): return lax.all_to_all(values, AXES, split_axis=0, concat_axis=0, tiled=True)  41 us
    pallas_call x2, Pallas kernels, body(): pl.pallas_call(sweep_kernel, out_shape=[values_shape, field], in_specs=[i...  3.11 us
    pallas_call x1, Pallas kernels, body(): pl.pallas_call(functools.partial(last_kernel, grid_size), out_shape=[jax....  1.88 us
    pallas_call x1, Pallas kernels, body(): pl.pallas_call(functools.partial(first_kernel, grid_size), out_shape=[val...  1.78 us

profile of v8, /device:TPU:0, one launch (start us, length us, event | category | flops | bytes accessed | tf_op | source)
XLA Modules:
  0.0 49.4 jit_solution(1476436508864130233)
XLA Ops:
  0.6 0.9 %pack_ends.1 = (f32[32,4,128]{2,1,0:T(4,128)S(1)}, f32[256,128]{1,0:T(8,128)S(1)}) custom-call(s32[2,16]{1,0:T(2,128)} %bitcast.10, s32[2,16]{1,0:T(2,128)} %bitcast.11, s32[16,2,64]{2,1,0:T(2,128)} %nodes_hbm.1, f32[16,64]{1,0:T(8,128)} %weight_hbm.1, f32[256,128]{1,0:T(8,128)} %bitcast.9), custom_call_target="tpu_custom_call" | custom-call | tf_op jit(solution)/shard_map/pack_ends/pallas_call | solution.py:386
  1.6 14.5 %all_to_all.20.message_ref = f32[32,4,128]{2,1,0:T(4,128)S(1)} all-to-all(f32[32,4,128]{2,1,0:T(4,128)S(1)} %get-tuple-element.21), channel_id=1, replica_groups=mesh['wide'=8,'narrow'=4] {'wide','narrow'}, dimensions={0} | all-to-all | bytes 131072 | tf_op jit(solution)/shard_map/all_to_all | solution.py:384
  16.1 1.8 %first_values.1 = (f32[32,1,128]{2,1,0:T(1,128)S(1)}, bf16[2,256,2048]{2,1,0:T(8,128)(2,1)S(1)}, bf16[2,128,2048]{2,1,0:T(8,128)(2,1)S(1)}, s32[2,16,128]{2,1,0:...) custom-call(f32[32,4,128]{2,1,0:T(4,128)S(1)} %all_to_all.20.message, ...), custom_call_target="tpu_custom_call" | custom-call | tf_op jit(solution)/shard_map/first_values/pallas_call | solution.py:405
  17.9 8.8 %all_to_all.21.arrived_ref = f32[32,1,128]{2,1,0:T(1,128)S(1)} all-to-all(f32[32,1,128]{2,1,0:T(1,128)S(1)} %get-tuple-element.23), channel_id=1, replica_groups=mesh['wide'=8,'narrow'=4] {'wide','narrow'}, dimensions={0} | all-to-all | bytes 32768 | tf_op jit(solution)/shard_map/all_to_all | solution.py:384
  26.7 1.6 %sweep.2 = (f32[32,1,128]{2,1,0:T(1,128)S(1)}, f32[256,128]{1,0:T(8,128)S(1)}) custom-call(f32[32,1,128]{2,1,0:T(1,128)S(1)} %all_to_all.21.arrived_ref, bf16[2,256,2048]{2,1,0:T(8,128)(2,1)S(1)} %get-tuple-element.24.row_hot_ref, bf16[2,128,2048]{2,1,0:T(8,128)(2,1)S(1)} %get-tuple-element.25.col_hot_ref, s32[2,16,128]{2,1,0:T(8,128)S(1)} %get-tuple-element.26.row_ref, ...), custom_call_target="tpu_custom_call" | custom-call | tf_op jit(solution)/shard_map/sweep/pallas_call | solution.py:425
  28.3 8.8 %all_to_all.22.arrived_ref = f32[32,1,128]{2,1,0:T(1,128)S(1)} all-to-all(f32[32,1,128]{2,1,0:T(1,128)S(1)} %get-tuple-element.33), channel_id=1, replica_groups=mesh['wide'=8,'narrow'=4] {'wide','narrow'}, dimensions={0} | all-to-all | bytes 32768 | tf_op jit(solution)/shard_map/all_to_all | solution.py:384
  37.1 1.6 %sweep.3 = (f32[32,1,128]{2,1,0:T(1,128)S(1)}, f32[256,128]{1,0:T(8,128)S(1)}) custom-call(f32[32,1,128]{2,1,0:T(1,128)S(1)} %all_to_all.22.arrived_ref, bf16[2,256,2048]{2,1,0:T(8,128)(2,1)S(1)} %get-tuple-element.24.row_hot_ref, bf16[2,128,2048]{2,1,0:T(8,128)(2,1)S(1)} %get-tuple-element.25.col_hot_ref, s32[2,16,128]{2,1,0:T(8,128)S(1)} %get-tuple-element.26.row_ref, ...), custom_call_target="tpu_custom_call" | custom-call | tf_op jit(solution)/shard_map/sweep/pallas_call | solution.py:425
  38.7 8.8 %all_to_all.23.arrived_ref = f32[32,1,128]{2,1,0:T(1,128)S(1)} all-to-all(f32[32,1,128]{2,1,0:T(1,128)S(1)} %get-tuple-element.35), channel_id=1, replica_groups=mesh['wide'=8,'narrow'=4] {'wide','narrow'}, dimensions={0} | all-to-all | bytes 32768 | tf_op jit(solution)/shard_map/all_to_all | solution.py:384
  47.6 1.9 %last_sweep.1 = (f32[256,128]{1,0:T(8,128)}, f32[256,128]{1,0:T(8,128)}) custom-call(f32[32,1,128]{2,1,0:T(1,128)S(1)} %all_to_all.23.arrived_ref, bf16[2,256,2048]{2,1,0:T(8,128)(2,1)S(1)} %get-tuple-element.24.row_hot_ref, bf16[2,128,2048]{2,1,0:T(8,128)(2,1)S(1)} %get-tuple-element.25.col_hot_ref, f32[2,16,128]{2,1,0:T(8,128)S(1)} %get-tuple-element.27.weight_ref, ...), custom_call_target="tpu_custom_call" | custom-call | tf_op jit(solution)/shard_map/last_sweep/pallas_call | solution.py:438

commit v9 on v7

--- a/solution.py
+++ b/solution.py
@@ -137,7 +137,7 @@
 def gather(col_hot_ref, row_ref, peer_ref, both_ref, values_ref, block):
     _, per_block, width = row_ref.shape
     rows = both_ref.shape[0]
-    group = 2
+    group = 4
     row_ids = lax.broadcasted_iota(jnp.int32, (rows, width), 0)
     both = both_ref[...]
     for start in range(0, per_block, group):

time: 49.7 us -> 49.7 us (level)
  no operation moved by 1% of the time
where the time goes in v9:
time: 49.7 us; the launch traced here: 49.4 us
  blocking collectives  41 us (82%)
  Pallas kernels  7.72 us (16%)
  between operations  0.66 us (1%)
    all_to_all x4, blocking collectives, exchange(): return lax.all_to_all(values, AXES, split_axis=0, concat_axis=0, tiled=True)  41 us
    pallas_call x2, Pallas kernels, body(): pl.pallas_call(sweep_kernel, out_shape=[values_shape, field], in_specs=[i...  3.11 us
    pallas_call x1, Pallas kernels, body(): pl.pallas_call(functools.partial(last_kernel, grid_size), out_shape=[jax....  1.87 us
    pallas_call x1, Pallas kernels, body(): pl.pallas_call(functools.partial(first_kernel, grid_size), out_shape=[val...  1.78 us

profile of v9, /device:TPU:0, one launch (start us, length us, event | category | flops | bytes accessed | tf_op | source)
XLA Modules:
  0.0 49.4 jit_solution(3300071214589810752)
XLA Ops:
  0.6 0.9 %pack_ends.1 = (f32[32,4,128]{2,1,0:T(4,128)S(1)}, f32[256,128]{1,0:T(8,128)S(1)}) custom-call(s32[2,16]{1,0:T(2,128)} %bitcast.10, s32[2,16]{1,0:T(2,128)} %bitcast.11, s32[16,2,64]{2,1,0:T(2,128)} %nodes_hbm.1, f32[16,64]{1,0:T(8,128)} %weight_hbm.1, f32[256,128]{1,0:T(8,128)} %bitcast.9), custom_call_target="tpu_custom_call" | custom-call | tf_op jit(solution)/shard_map/pack_ends/pallas_call | solution.py:383
  1.6 14.5 %all_to_all.20.message_ref = f32[32,4,128]{2,1,0:T(4,128)S(1)} all-to-all(f32[32,4,128]{2,1,0:T(4,128)S(1)} %get-tuple-element.21), channel_id=1, replica_groups=mesh['wide'=8,'narrow'=4] {'wide','narrow'}, dimensions={0} | all-to-all | bytes 131072 | tf_op jit(solution)/shard_map/all_to_all | solution.py:381
  16.1 1.8 %first_values.1 = (f32[32,1,128]{2,1,0:T(1,128)S(1)}, bf16[2,256,2048]{2,1,0:T(8,128)(2,1)S(1)}, bf16[2,128,2048]{2,1,0:T(8,128)(2,1)S(1)}, s32[2,16,128]{2,1,0:...) custom-call(f32[32,4,128]{2,1,0:T(4,128)S(1)} %all_to_all.20.message, ...), custom_call_target="tpu_custom_call" | custom-call | tf_op jit(solution)/shard_map/first_values/pallas_call | solution.py:402
  17.9 8.8 %all_to_all.21.arrived_ref = f32[32,1,128]{2,1,0:T(1,128)S(1)} all-to-all(f32[32,1,128]{2,1,0:T(1,128)S(1)} %get-tuple-element.23), channel_id=1, replica_groups=mesh['wide'=8,'narrow'=4] {'wide','narrow'}, dimensions={0} | all-to-all | bytes 32768 | tf_op jit(solution)/shard_map/all_to_all | solution.py:381
  26.7 1.6 %sweep.2 = (f32[32,1,128]{2,1,0:T(1,128)S(1)}, f32[256,128]{1,0:T(8,128)S(1)}) custom-call(f32[32,1,128]{2,1,0:T(1,128)S(1)} %all_to_all.21.arrived_ref, bf16[2,256,2048]{2,1,0:T(8,128)(2,1)S(1)} %get-tuple-element.24.row_hot_ref, bf16[2,128,2048]{2,1,0:T(8,128)(2,1)S(1)} %get-tuple-element.25.col_hot_ref, s32[2,16,128]{2,1,0:T(8,128)S(1)} %get-tuple-element.26.row_ref, ...), custom_call_target="tpu_custom_call" | custom-call | tf_op jit(solution)/shard_map/sweep/pallas_call | solution.py:422
  28.3 8.8 %all_to_all.22.arrived_ref = f32[32,1,128]{2,1,0:T(1,128)S(1)} all-to-all(f32[32,1,128]{2,1,0:T(1,128)S(1)} %get-tuple-element.33), channel_id=1, replica_groups=mesh['wide'=8,'narrow'=4] {'wide','narrow'}, dimensions={0} | all-to-all | bytes 32768 | tf_op jit(solution)/shard_map/all_to_all | solution.py:381
  37.1 1.6 %sweep.3 = (f32[32,1,128]{2,1,0:T(1,128)S(1)}, f32[256,128]{1,0:T(8,128)S(1)}) custom-call(f32[32,1,128]{2,1,0:T(1,128)S(1)} %all_to_all.22.arrived_ref, bf16[2,256,2048]{2,1,0:T(8,128)(2,1)S(1)} %get-tuple-element.24.row_hot_ref, bf16[2,128,2048]{2,1,0:T(8,128)(2,1)S(1)} %get-tuple-element.25.col_hot_ref, s32[2,16,128]{2,1,0:T(8,128)S(1)} %get-tuple-element.26.row_ref, ...), custom_call_target="tpu_custom_call" | custom-call | tf_op jit(solution)/shard_map/sweep/pallas_call | solution.py:422
  38.7 8.8 %all_to_all.23.arrived_ref = f32[32,1,128]{2,1,0:T(1,128)S(1)} all-to-all(f32[32,1,128]{2,1,0:T(1,128)S(1)} %get-tuple-element.35), channel_id=1, replica_groups=mesh['wide'=8,'narrow'=4] {'wide','narrow'}, dimensions={0} | all-to-all | bytes 32768 | tf_op jit(solution)/shard_map/all_to_all | solution.py:381
  47.6 1.9 %last_sweep.1 = (f32[256,128]{1,0:T(8,128)}, f32[256,128]{1,0:T(8,128)}) custom-call(f32[32,1,128]{2,1,0:T(1,128)S(1)} %all_to_all.23.arrived_ref, bf16[2,256,2048]{2,1,0:T(8,128)(2,1)S(1)} %get-tuple-element.24.row_hot_ref, bf16[2,128,2048]{2,1,0:T(8,128)(2,1)S(1)} %get-tuple-element.25.col_hot_ref, f32[2,16,128]{2,1,0:T(8,128)S(1)} %get-tuple-element.27.weight_ref, ...), custom_call_target="tpu_custom_call" | custom-call | tf_op jit(solution)/shard_map/last_sweep/pallas_call | solution.py:435
